TPU v7x, 32 devices: a whole 2x2x4 slice. The times are simulated.
32 devices in a mesh: slab: 8 (over y, x, core), chan: 4 (over z).
Axes of the slice: x: 2, y: 2, z: 4, core: 2. Of those that a mesh axis runs over, the one named last changes fastest.
Arguments:
- inputs: bfloat16 [256, 16, 1536], P('chan', 'slab'), may hold values from -6 to 6
- filters: bfloat16 [27, 256, 256], P(None, 'chan'), may hold values from -0.078125 to 0.078125
- cotangent: bfloat16 [256, 16, 1536], P('chan', 'slab'), may hold values from -6 to 6
Outputs:
- features: bfloat16 [256, 16, 1536], P('chan', 'slab')
- input_grad: bfloat16 [256, 16, 1536], P('chan', 'slab')
- filter_grad: float32 [27, 256, 256], P(None, 'chan', 'slab')
All inputs are finite; a program needn't handle non-finite values.
Results may differ from a plain program's by a relative error of at most 0.001.
Values may be sent and summed in bfloat16 or wider, within the bound.
A program may use at most 128 MiB of HBM per device.

v0:
```python
import math

import jax
import jax.numpy as jnp
from jax import lax
from jax.sharding import PartitionSpec as P

W = 64


offsets = (-1, 0, 1)


def padded(cells, sides, width):
    for axis, dim in sides:
        count = lax.axis_size(axis)
        head = lax.slice_in_dim(cells, 0, width, axis=dim)
        tail = lax.slice_in_dim(cells, cells.shape[dim] - width, cells.shape[dim], axis=dim)
        cells = jnp.concatenate(
            [
                lax.ppermute(tail, axis, [(i, (i + 1) % count) for i in range(count)]),
                cells,
                lax.ppermute(head, axis, [((i + 1) % count, i) for i in range(count)]),
            ],
            axis=dim,
        )
    return cells


def roll_cells(values, row_shift, column_shift):
    row_width = W
    length = values.shape[-1]
    column = lax.broadcasted_iota(jnp.int32, (length,), 0) % row_width
    if column_shift == 1:
        values = jnp.where(
            column == 0, jnp.roll(values, 1 - row_width, axis=-1), jnp.roll(values, 1, axis=-1)
        )
    elif column_shift == -1:
        values = jnp.where(
            column == row_width - 1,
            jnp.roll(values, row_width - 1, axis=-1),
            jnp.roll(values, -1, axis=-1),
        )
    if row_shift != 0:
        values = jnp.roll(values, row_shift * row_width, axis=-1)
    return values


def add_rims(stacked):
    return padded(stacked, (("slab", 2),), 1)


def local(inputs, filters, cotangent):
    planes = inputs.shape[1]
    flat_cells = inputs.shape[2]
    factor = 1.0 / math.sqrt(planes * lax.axis_size("slab") * flat_cells)
    rimmed = add_rims(jnp.stack([inputs, cotangent]))
    inputs_wide = lax.all_gather(rimmed[0], "chan", axis=0, tiled=True)
    grads_rims = rimmed[1]
    rolled_rims = jnp.stack(
        [
            roll_cells(grads_rims, row_shift, column_shift)
            for row_shift in offsets
            for column_shift in offsets
        ]
    )
    rolled = rolled_rims[:, :, 1 : 1 + planes]
    result = jnp.zeros((filters.shape[1], planes, flat_cells), jnp.float32)
    blocks = []
    for plane_shift in offsets:
        window = inputs_wide[:, plane_shift + 1 : plane_shift + 1 + planes]
        tap_rows = filters[9 * (plane_shift + 1) : 9 * (plane_shift + 2)]
        partial_value = jnp.einsum(
            "koc,cdp->kodp", tap_rows, window, preferred_element_type=jnp.float32
        )
        for row_shift in offsets:
            for column_shift in offsets:
                result = result + roll_cells(
                    partial_value[3 * (row_shift + 1) + column_shift + 1], -row_shift, -column_shift
                )
        blocks.append(
            jnp.einsum("kodp,cdp->koc", rolled, window, preferred_element_type=jnp.float32)
        )
    features = result.astype(jnp.bfloat16)
    filter_local = jnp.concatenate(blocks, 0) * factor
    filter_grad = lax.psum_scatter(filter_local, "slab", scatter_dimension=2, tiled=True)
    stacked = jnp.concatenate(
        [rolled_rims[:, :, 1 - plane_shift : 1 - plane_shift + planes] for plane_shift in offsets],
        0,
    )
    tap_rows = filters
    gradient = lax.psum_scatter(
        jnp.einsum("koc,kodp->cdp", tap_rows, stacked, preferred_element_type=jnp.float32),
        "chan",
        scatter_dimension=0,
        tiled=True,
    )
    input_grad = gradient.astype(jnp.bfloat16)
    return (features, input_grad, filter_grad)


def solution(mesh):
    placed = (P("chan", "slab", None), P(None, "chan", None), P("chan", "slab", None))
    return jax.shard_map(
        local,
        mesh=mesh,
        in_specs=placed,
        out_specs=(P("chan", "slab", None), P("chan", "slab", None), P(None, "chan", "slab")),
        check_vma=False,
    )
```

profile of v0, /device:TPU:0, one launch (start us, length us, event | category | flops | bytes accessed | tf_op | source)
XLA Modules:
  0.0 297.5 jit_solution(13978400101111446546)
XLA Ops:
  7.2 1.2 copy_bitcast_fusion
  9.0 2.9 collective-permute-start.1
  13.2 5.7 %collective-permute-done = bf16[2,64,1,1536]{3,1,2,0:T(8,128)(2,1)S(1)} collective-permute-done((bf16[2,64,1,1536]{3,1,2,0:T(8,128)(2,1)S(1)}, bf16[2,64,1,1536]{3,1,2,0:T(8,128)(2,1)S(1)}, u32[]{:S(2)}, u32[]{:S(2)}) %collective-permute-start) | collective-permute-done | bytes 393248 | tf_op jit(solution)/shard_map/ppermute | solution.py:21
  18.9 1.5 collective-permute-done.1
  23.6 1.2 fusion.67
  27.9 1.4 fusion.47
  29.3 1.3 slice_dynamic-update-slice_fusion
  30.7 1.4 fusion.48
  32.1 1.2 fusion.49
  33.3 1.2 fusion.50
  34.5 1.2 fusion.51
  35.8 5.0 %fusion.65 = (bf16[9,64,2,1536]{3,1,2,0:T(8,128)(2,1)S(1)}, bf16[9,64,2,1536]{3,1,2,0:T(8,128)(2,1)S(1)}, bf16[9,64,2,1536]{3,1,2,0:T(8,128)(2,1)S(1)}) fusion(bf16[9,64,4,1536]{3,1,2,0:T(8,128)(2,1)} %fusion.51), kind=kLoop, calls=%fused_computation.144 | loop fusion | bytes 21233664 | tf_op jit(solution)/shard_map/slice | solution.py:88
  40.8 4.9 %fusion.6 = f32[256,2,1536]{0,2,1:T(8,128)} fusion(bf16[9,64,2,1536]{3,1,2,0:T(8,128)(2,1)S(1)} %get-tuple-element.13, bf16[9,64,2,1536]{3,1,2,0:T(8,128)(2,1)S(1)} %get-tuple-element.14, bf16[9,64,2,1536]{3,1,2,0:T(8,128)(2,1)S(1)} %get-tuple-element.12, bf16[27,64,256]{2,1,0:T(8,128)(2,1)S(1)} %copy-done.26), kind=kOutput, calls=%fused_computation.9 | convolution fusion | flops 2728525824 | bytes 14647296 | tf_op jit(solution)/shard_map/koc,kodp->cdp/dot_general | solution.py:93
  45.7 4.3 %copy.56 = f32[256,2,1536]{2,1,0:T(2,128)S(1)} copy(f32[256,2,1536]{0,2,1:T(8,128)} %fusion.6) | data formatting | bytes 6291456 | tf_op jit(solution)/shard_map/koc,kodp->cdp/dot_general | solution.py:93
  50.0 149.7 %all-reduce.2 = bf16[256,2,1536]{2,1,0:T(2,128)(2,1)} all-reduce(f32[256,2,1536]{2,1,0:T(2,128)S(1)} %copy.56), channel_id=3, replica_groups=mesh['slab'=8,'chan'=4] {'chan'}, use_global_device_ids=true, to_apply=%region_0.1.clone | all-reduce | flops 786432 | bytes 4718592
  199.7 2.0 dynamic-slice_convert_fusion
  201.7 3.7 %fusion.14 = f32[9,64,256]{2,1,0:T(8,128)S(1)} fusion(bf16[9,64,4,1536]{3,1,2,0:T(8,128)(2,1)} %fusion.51, bf16[256,4,1536]{2,0,1:T(8,128)(2,1)} %bitcast.272), kind=kOutput, calls=%fused_computation.19 | convolution fusion | flops 905969664 | bytes 9240576 | tf_op jit(solution)/shard_map/kodp,cdp->koc/dot_general | solution.py:82
  205.4 3.1 %convolution_bitcast_fusion.4 = f32[9,64,256]{2,1,0:T(8,128)S(1)} fusion(bf16[9,64,4,1536]{3,1,2,0:T(8,128)(2,1)} %fusion.51, bf16[256,4,1536]{2,0,1:T(8,128)(2,1)S(1)} %bitcast.273), kind=kOutput, calls=%fused_computation.21 | convolution fusion | flops 905969664 | bytes 9240576 | tf_op jit(solution)/shard_map/kodp,cdp->koc/dot_general | solution.py:82
  208.6 3.2 %convolution_bitcast_fusion.3 = f32[9,64,256]{2,1,0:T(8,128)S(1)} fusion(bf16[9,64,4,1536]{3,1,2,0:T(8,128)(2,1)} %fusion.51, bf16[256,4,1536]{2,0,1:T(8,128)(2,1)S(1)} %bitcast.274), kind=kOutput, calls=%fused_computation.20 | convolution fusion | flops 905969664 | bytes 9240576 | tf_op jit(solution)/shard_map/kodp,cdp->koc/dot_general | solution.py:82
  215.7 2.5 slice_bitcast_fusion.24
  218.2 2.1 slice.758
  220.5 2.5 slice_bitcast_fusion.15
  223.0 1.3 slice.776
  224.4 1.2 slice.804
  225.7 2.0 slice_bitcast_fusion.6
  227.7 1.2 slice.850
  230.2 1.4 maximum_multiply_fusion
  231.6 5.5 %copy.57 = f32[27,64,256]{1,0,2:T(8,128)} copy(f32[27,64,256]{2,1,0:T(8,128)} %maximum_multiply_fusion) | data formatting | bytes 3538944 | tf_op jit(solution)/shard_map/mul | solution.py:85
  237.2 3.8 %maximum_select_fusion.17 = (f32[64,2,1536]{2,0,1:T(8,128)S(1)}, f32[64,2,1536]{2,0,1:T(8,128)S(1)}, f32[64,2,1536]{2,0,1:T(8,128)S(1)}, f32[64,2,1536]{2,0,1:T(8,128)S(1)}) fusion(f32[64,2,1473]{2,0,1:T(8,128)} %bitcast.271, f32[64,2,63]{2,0,1:T(8,128)} %slice.848, f32[64,2,1]{2,0,1:T(8,128)} %slice.851, f32[64,2,1535]{2,0,1:T(8,128)} %slice.850, ...), kind=kLoop, calls=%fused_computation.96 | loop fusion | flops 2359296 | bytes 9438720 | tf_op jit(solution)/shard_map/jit(_where)/select_n | solution.py:39
  263.1 7.1 %fusion.23 = bf16[64,2,1536]{2,0,1:T(8,128)(2,1)S(1)} fusion(f32[9,64,2,1536]{3,1,2,0:T(8,128)} %copy-done.2, f32[9,64,2,1536]{3,1,2,0:T(8,128)} %copy-done.1, f32[9,64,2,1536]{3,1,0,2:T(8,128)} %copy-done, f32[64,2,1472]{2,0,1:T(8,128)S(1)} %bitcast.284, f32[64,2,64]{2,0,1:T(8,128)S(1)} %slice.722, f32[64,2,1472]{2,0,1:T(8,128)S(1)} %bitcast.278, ...), kind=kLoop, calls=%fused_computation.33 | loop fusion | flops 12386304 | bytes 26348544 | tf_op jit(solution)/shard_map/convert_element_type | solution.py:84
  271.4 17.2 %reduce-scatter.2.cloned.1.call-done = f32[27,64,32]{1,0,2:T(8,128)} async-done(((f32[27,64,256]{1,0,2:T(8,128)}), f32[27,64,32]{1,0,2:T(8,128)}) %reduce-scatter.2.cloned.1.call-update) | async-done | bytes 221200 | tf_op jit(solution)/shard_map/reduce_scatter | solution.py:86
  288.6 2.1 copy.59
  (168 shorter events, 36.1 us)
Async XLA Ops:
  7.2 4.8 %copy-start.28 = (u32[32]{0:T(128)S(1)}, u32[32]{0:T(128)}, u32[]{:S(2)}) copy-start(u32[32]{0:T(128)} %constant.93) | copy-start | bytes 388
  7.2 194.5 %all-gather.3.cloned.1.call-start = ((), (), s32[]{:S(2)}) async-start(), calls=%async_computation.2 | async-start | bytes 3932160 | tf_op jit(solution)/shard_map/all_gather | solution.py:58
  8.5 10.4 %collective-permute-start = (bf16[2,64,1,1536]{3,1,2,0:T(8,128)(2,1)S(1)}, bf16[2,64,1,1536]{3,1,2,0:T(8,128)(2,1)S(1)}, u32[]{:S(2)}, u32[]{:S(2)}) collective-permute-start(bf16[2,64,1,1536]{3,1,2,0:T(8,128)(2,1)S(1)} %get-tuple-element.69), channel_id=1, source_target_pairs={{0,4},{4,8},{8,12},{12,16},{16,20},{20,24},{24,28},{28,0},{1,5},{5... | collective-permute-start | bytes 1179656 | tf_op jit(solution)/shard_map/ppermute | solution.py:21
  9.0 11.4 %collective-permute-start.1 = (bf16[2,64,1,1536]{3,1,2,0:T(8,128)(2,1)S(1)}, bf16[2,64,1,1536]{3,1,2,0:T(8,128)(2,1)S(1)}, u32[]{:S(2)}, u32[]{:S(2)}) collective-permute-start(bf16[2,64,1,1536]{3,1,2,0:T(8,128)(2,1)S(1)} %get-tuple-element.70), channel_id=1, source_target_pairs={{4,0},{8,4},{12,8},{16,12},{20,16},{24,20},{28,24},{0,28},{5,1},{9... | collective-permute-start | bytes 1179656 | tf_op jit(solution)/shard_map/ppermute | solution.py:23
  30.6 257.9 %reduce-scatter.2.cloned.1.call-start = ((), (), s32[]{:S(2)}) async-start(), calls=%async_computation.1 | async-start | bytes 4718592 | tf_op jit(solution)/shard_map/reduce_scatter | solution.py:86
  30.7 3.9 %copy-start.24 = (bf16[64,4,1472]{2,0,1:T(8,128)(2,1)S(1)}, bf16[64,4,1472]{2,0,1:T(8,128)(2,1)}, u32[]{:S(2)}) copy-start(bf16[64,4,1472]{2,0,1:T(8,128)(2,1)} %get-tuple-element.43) | copy-start | bytes 2260996
  35.8 5.0 %copy-start.26 = (bf16[27,64,256]{2,1,0:T(8,128)(2,1)S(1)}, bf16[27,64,256]{2,1,0:T(8,128)(2,1)}, u32[]{:S(2)}) copy-start(bf16[27,64,256]{2,1,0:T(8,128)(2,1)} %param.4) | copy-start | bytes 2654212
  201.7 3.7 %copy-start.17 = (bf16[1,256,4,1536]{3,1,2,0:T(8,128)(2,1)S(1)}, bf16[1,256,4,1536]{3,1,2,0:T(8,128)(2,1)}, u32[]{:S(2)}) copy-start(bf16[1,256,4,1536]{3,1,2,0:T(8,128)(2,1)} %all-gather.3.cloned.1.call-done) | copy-start | bytes 9437188
  208.5 3.2 %copy-start.27 = (bf16[27,64,256]{2,1,0:T(8,128)(2,1)S(1)}, bf16[27,64,256]{2,1,0:T(8,128)(2,1)}, u32[]{:S(2)}) copy-start(bf16[27,64,256]{2,1,0:T(8,128)(2,1)} %param.4) | copy-start | bytes 2654212
  212.8 2.8 copy-start
  213.9 6.5 %copy-start.1 = (f32[9,64,2,1536]{3,1,2,0:T(8,128)}, f32[9,64,2,1536]{3,1,2,0:T(8,128)S(1)}, u32[]{:S(2)}) copy-start(f32[9,64,2,1536]{3,1,2,0:T(8,128)S(1)} %convolution_bitcast_fusion.1) | copy-start | bytes 21233668
  215.7 10.0 %copy-start.2 = (f32[9,64,2,1536]{3,1,2,0:T(8,128)}, f32[9,64,2,1536]{3,1,2,0:T(8,128)S(1)}, u32[]{:S(2)}) copy-start(f32[9,64,2,1536]{3,1,2,0:T(8,128)S(1)} %convolution_bitcast_fusion) | copy-start | bytes 21233668
  218.2 4.7 %copy-start.13 = (f32[64,2,1536]{2,0,1:T(8,128)}, f32[64,2,1536]{2,0,1:T(8,128)S(1)}, u32[]{:S(2)}) copy-start(f32[64,2,1536]{2,0,1:T(8,128)S(1)} %get-tuple-element.31) | copy-start | bytes 2359300
  223.0 4.7 %copy-start.14 = (f32[64,2,1536]{2,0,1:T(8,128)}, f32[64,2,1536]{2,0,1:T(8,128)S(1)}, u32[]{:S(2)}) copy-start(f32[64,2,1536]{2,0,1:T(8,128)S(1)} %get-tuple-element.23) | copy-start | bytes 2359300
  223.0 4.7 %copy-start.15 = (f32[64,2,1536]{2,0,1:T(8,128)}, f32[64,2,1536]{2,0,1:T(8,128)S(1)}, u32[]{:S(2)}) copy-start(f32[64,2,1536]{2,0,1:T(8,128)S(1)} %get-tuple-element.28) | copy-start | bytes 2359300
  227.7 1.9 copy-start.16
  241.0 1.5 copy-start.11
  241.5 1.3 copy-start.10
  241.8 1.5 copy-start.12
  246.0 1.2 copy-start.4
  246.3 1.3 copy-start.3
  246.7 1.9 copy-start.18
  247.1 2.4 copy-start.6
  247.5 3.7 %copy-start.5 = (f32[64,2,1536]{2,0,1:T(8,128)S(1)}, f32[64,2,1536]{2,0,1:T(8,128)}, u32[]{:S(2)}) copy-start(f32[64,2,1536]{2,0,1:T(8,128)} %get-tuple-element.26) | copy-start | bytes 2359300
  247.9 4.9 %copy-start.19 = (f32[64,2,1536]{2,0,1:T(8,128)S(1)}, f32[64,2,1536]{2,0,1:T(8,128)}, u32[]{:S(2)}) copy-start(f32[64,2,1536]{2,0,1:T(8,128)} %get-tuple-element.24) | copy-start | bytes 2359300
  248.9 4.8 %copy-start.8 = (f32[64,2,1536]{2,0,1:T(8,128)S(1)}, f32[64,2,1536]{2,0,1:T(8,128)}, u32[]{:S(2)}) copy-start(f32[64,2,1536]{2,0,1:T(8,128)} %get-tuple-element.19) | copy-start | bytes 2359300
  249.8 5.5 %copy-start.7 = (f32[64,2,1536]{2,0,1:T(8,128)S(1)}, f32[64,2,1536]{2,0,1:T(8,128)}, u32[]{:S(2)}) copy-start(f32[64,2,1536]{2,0,1:T(8,128)} %get-tuple-element.18) | copy-start | bytes 2359300
  251.4 5.5 %copy-start.20 = (f32[64,2,1536]{2,0,1:T(8,128)S(1)}, f32[64,2,1536]{2,0,1:T(8,128)}, u32[]{:S(2)}) copy-start(f32[64,2,1536]{2,0,1:T(8,128)} %get-tuple-element.16) | copy-start | bytes 2359300
  260.7 2.2 copy-start.21
  260.7 2.3 copy-start.22
  260.7 2.3 copy-start.23
  260.7 2.4 copy-start.25
  (1 other events, 1.1 us)
Sparse Core Ops, SparseCore 0:
  30.7 102.5 all-gather.2
  237.3 51.2 reduce-scatter.1
where the time goes:
time: 298 us; the launch traced here: 297 us
  blocking collectives  150 us (50%)
  local copies, waits for them, and re-layouts  61.1 us (21%)
  other arithmetic  25.2 us (8%)
  waiting for transfers between devices  24.4 us (8%)
  matrix products  18.2 us (6%)
  between operations  15.3 us (5%)
  starting transfers between devices  3.53 us (1%)
    unnamed x1, blocking collectives  150 us
    reduce_scatter x1, waiting for transfers between devices, local(): lax.psum_scatter(filter_local, 'slab', scatter_dimension=2, tiled=True)  17.2 us
    slice x33, local copies, waits for them, and re-layouts, roll_cells(): values = jnp.roll(values, row_shift * row_width, axis=-1)  10.7 us
    dot_general x3, matrix products, local(): jnp.einsum('kodp,cdp->koc', rolled, window, preferred_element_type=jnp.fl...  10 us
    slice x18, local copies, waits for them, and re-layouts, roll_cells(): jnp.roll(values, -1, axis=-1)  9.76 us
    unnamed x7, other arithmetic  8.26 us
    convert_element_type x1, other arithmetic, local(): features = result.astype(jnp.bfloat16)  7.07 us
    squeeze x3, local copies, waits for them, and re-layouts, local(): partial_value[3 * (row_shift + 1) + column_shift + 1]  7 us
  transfers between devices with their start and end apart: 4, of which 3 were waited for; matrix products, arithmetic and copies ran while one was open for 19% of the time, Pallas kernels for 0%

commit v1 on v0

v1 whole, which is shorter than its diff:
```python
import functools
import math

import jax
import jax.numpy as jnp
from jax import lax
from jax.experimental import pallas as pl
from jax.experimental.pallas import tpu as pltpu
from jax.sharding import PartitionSpec as P

W = 64
MESH = pl.DeviceIdType.MESH
F32 = jnp.float32
BF16 = jnp.bfloat16


def turn_and_shift(src, dst):
    planes, channels, cells = src.shape
    for s in range(planes):

        def step(m, carry):
            turned = src[s, :, pl.ds(pl.multiple_of(m * 128, 128), 128)].astype(F32).T
            for h in range(128 // W):
                row = turned[h * W : (h + 1) * W]
                at = pl.ds(pl.multiple_of(m * 128 + (h + 1) * W, W), W)
                dst[0, s, at, :] = pltpu.roll(row, 1, 0).astype(BF16)
                dst[1, s, at, :] = row.astype(BF16)
                dst[2, s, at, :] = pltpu.roll(row, W - 1, 0).astype(BF16)
            return carry

        lax.fori_loop(0, cells // 128, step, 0)
        for r in range(3):
            dst[r, s, 0:W, :] = dst[r, s, cells : cells + W, :]
            dst[r, s, cells + W : cells + 2 * W, :] = dst[r, s, W : 2 * W, :]


def conv(src, weights, y):
    planes, rows, cells = y.shape
    chunk = 512
    for s in range(planes):

        def step(n, carry):
            total = None
            for q in range(3):
                for r in range(3):
                    part = jnp.dot(
                        src[r, s, pl.ds(pl.multiple_of(n * chunk + q * W, W), chunk), :],
                        weights[3 * q + r],
                        preferred_element_type=F32,
                    )
                    total = part if total is None else total + part
            y[s, :, pl.ds(pl.multiple_of(n * chunk, chunk), chunk)] = total.T
            return carry

        lax.fori_loop(0, cells // chunk, step, 0)


def finish(y, rim, out):
    planes = y.shape[0]
    ch = out.shape[1]
    for d in range(planes):
        total = y[d, ch : 2 * ch, :]
        total = total + (y[d - 1, 0:ch, :] if d > 0 else rim[0])
        total = total + (y[d + 1, 2 * ch : 3 * ch, :] if d < planes - 1 else rim[1])
        out[d] = total.astype(out.dtype)


def kernel(
    S, C, factor,
    x, g, wf, wt,
    feat, igrad, dw,
    xg, gg, wg, xt, gt, yx, yg, g3, grim, xrim, irim, dwt, dwr,
    own_sem, x_s, x_r, g_s, g_r, w_s, w_r, gr_s, gr_r, xr_s, xr_r, ir_s, ir_r, d_s, d_r,
):
    planes, ch, cells = x.shape
    cs = dwt.shape[1] // S
    me_s = lax.axis_index("slab")
    me_c = lax.axis_index("chan")

    barrier = pltpu.get_barrier_semaphore()
    for k in range(1, S):
        pl.semaphore_signal(barrier, inc=1, device_id={"slab": lax.rem(me_s + k, S)}, device_id_type=MESH)
    for k in range(1, C):
        pl.semaphore_signal(barrier, inc=1, device_id={"chan": lax.rem(me_c + k, C)}, device_id_type=MESH)
    pl.semaphore_wait(barrier, S - 1 + C - 1)

    mine = pl.ds(pl.multiple_of(me_c * ch, ch), ch)

    def to_chan(k, src, dst, send, recv):
        return pltpu.make_async_remote_copy(
            src_ref=src, dst_ref=dst, send_sem=send.at[k - 1], recv_sem=recv.at[k - 1],
            device_id={"chan": lax.rem(me_c + k, C)}, device_id_type=MESH,
        )

    def to_slab(k, src, dst, send, recv, slot):
        return pltpu.make_async_remote_copy(
            src_ref=src, dst_ref=dst, send_sem=send.at[slot], recv_sem=recv.at[slot],
            device_id={"slab": lax.rem(me_s + k, S)}, device_id_type=MESH,
        )

    def rims(low, high, dst, send, recv):
        return [
            to_slab(1, high, dst.at[0], send, recv, 0),
            to_slab(S - 1, low, dst.at[1], send, recv, 1),
        ]

    x_copies = [to_chan(k, x, xg.at[:, mine, :], x_s, x_r) for k in range(1, C)]
    for c in x_copies:
        c.start()
    g_rims = rims(g.at[0], g.at[planes - 1], grim, gr_s, gr_r)
    for c in g_rims:
        c.start()
    own = [
        pltpu.make_async_copy(x, xg.at[:, mine, :], own_sem.at[0]),
        pltpu.make_async_copy(g, gg.at[:, mine, :], own_sem.at[1]),
        pltpu.make_async_copy(wt.at[me_c], wg.at[:, mine, :], own_sem.at[2]),
    ]
    for c in own:
        c.start()
    for c in own:
        c.wait()
    for c in x_copies:
        c.wait_send()
    g_copies = [to_chan(k, g, gg.at[:, mine, :], g_s, g_r) for k in range(1, C)]
    w_copies = [
        to_chan(k, wt.at[lax.rem(me_c + k, C)], wg.at[:, mine, :], w_s, w_r) for k in range(1, C)
    ]
    for c in g_copies + w_copies:
        c.start()
    for c in g_rims:
        c.wait()
    for s in range(planes):
        for p in range(3):
            d = s - (p - 1)
            plane = grim[0] if d < 0 else grim[1] if d >= planes else g[d]
            g3[s, p * ch : (p + 1) * ch, :] = plane
    for c in x_copies:
        c.wait_recv()

    turn_and_shift(xg, xt)

    def weight_step(t, carry):
        total = None
        for s in range(planes):
            part = jnp.dot(
                g3[s],
                xt[lax.rem(t, 3), s, pl.ds(pl.multiple_of(lax.div(t, 3) * W, W), cells), :],
                preferred_element_type=F32,
            )
            total = part if total is None else total + part
        dwt[t] = total.T
        return carry

    lax.fori_loop(0, 9, weight_step, 0)
    d_copies = [
        to_slab(
            k,
            dwt.at[:, pl.ds(pl.multiple_of(lax.rem(me_s + k, S) * cs, cs), cs), :],
            dwr.at[k - 1], d_s, d_r, k - 1,
        )
        for k in range(1, S)
    ]
    for c in d_copies:
        c.start()
    conv(xt, wf, yx)
    x_rims = rims(yx.at[0, 2 * ch : 3 * ch, :], yx.at[planes - 1, 0:ch, :], xrim, xr_s, xr_r)
    for c in x_rims:
        c.start()

    for c in g_copies + w_copies:
        c.wait()
    turn_and_shift(gg, gt)
    conv(gt, wg, yg)
    i_rims = rims(yg.at[0, 2 * ch : 3 * ch, :], yg.at[planes - 1, 0:ch, :], irim, ir_s, ir_r)
    for c in i_rims:
        c.start()
    for c in x_rims:
        c.wait()
    finish(yx, xrim, feat)
    for c in d_copies:
        c.wait()
    total = dwt[:, pl.ds(pl.multiple_of(me_s * cs, cs), cs), :]
    for k in range(S - 1):
        total = total + dwr[k]
    dw[...] = total * factor
    for c in i_rims:
        c.wait()
    finish(yg, irim, igrad)


def local(inputs, filters, cotangent):
    S = lax.axis_size("slab")
    C = lax.axis_size("chan")
    ch, planes, cells = inputs.shape
    wide = C * ch
    cs = wide // S
    factor = 1.0 / math.sqrt(planes * S * cells)
    x = inputs.transpose(1, 0, 2)
    g = cotangent.transpose(1, 0, 2)
    taps = filters.reshape(3, 9, ch, wide)
    wf = taps.transpose(1, 3, 0, 2).reshape(9, wide, 3 * ch)
    back = filters[::-1].reshape(3, 9, ch, C, ch)
    wt = back.transpose(3, 1, 2, 0, 4).reshape(C, 9, ch, 3 * ch)
    dma = pltpu.SemaphoreType.DMA
    vmem = pl.BlockSpec(memory_space=pltpu.VMEM)
    feat, igrad, dw = pl.pallas_call(
        functools.partial(kernel, S, C, factor),
        out_shape=(
            jax.ShapeDtypeStruct((planes, ch, cells), BF16),
            jax.ShapeDtypeStruct((planes, ch, cells), BF16),
            jax.ShapeDtypeStruct((9, cs, 3 * ch), F32),
        ),
        in_specs=[vmem] * 4,
        out_specs=[vmem] * 3,
        scratch_shapes=[
            pltpu.VMEM((planes, wide, cells), BF16),
            pltpu.VMEM((planes, wide, cells), BF16),
            pltpu.VMEM((9, wide, 3 * ch), BF16),
            pltpu.VMEM((3, planes, cells + 2 * W, wide), BF16),
            pltpu.VMEM((3, planes, cells + 2 * W, wide), BF16),
            pltpu.VMEM((planes, 3 * ch, cells), F32),
            pltpu.VMEM((planes, 3 * ch, cells), F32),
            pltpu.VMEM((planes, 3 * ch, cells), BF16),
            pltpu.VMEM((2, ch, cells), BF16),
            pltpu.VMEM((2, ch, cells), F32),
            pltpu.VMEM((2, ch, cells), F32),
            pltpu.VMEM((9, wide, 3 * ch), F32),
            pltpu.VMEM((S - 1, 9, cs, 3 * ch), F32),
            dma((3,)),
            dma((C - 1,)), dma((C - 1,)),
            dma((C - 1,)), dma((C - 1,)),
            dma((C - 1,)), dma((C - 1,)),
            dma((2,)), dma((2,)),
            dma((2,)), dma((2,)),
            dma((2,)), dma((2,)),
            dma((S - 1,)), dma((S - 1,)),
        ],
        compiler_params=pltpu.CompilerParams(
            collective_id=0, has_side_effects=True, vmem_limit_bytes=48 * 1024 * 1024
        ),
    )(x, g, wf, wt)
    filter_grad = dw.reshape(3, 3, cs, 3, ch).transpose(3, 0, 1, 4, 2).reshape(27, ch, cs)
    return (feat.transpose(1, 0, 2), igrad.transpose(1, 0, 2), filter_grad)


def solution(mesh):
    placed = (P("chan", "slab", None), P(None, "chan", None), P("chan", "slab", None))
    return jax.shard_map(
        local,
        mesh=mesh,
        in_specs=placed,
        out_specs=(P("chan", "slab", None), P("chan", "slab", None), P(None, "chan", "slab")),
        check_vma=False,
    )
```

time: 298 us -> 135 us (0.45)
  the two profiles are of different devices: /device:TPU:0 before, /device:TPU:9 now
where the time goes in v1:
time: 135 us
  Pallas kernels  115 us (85%)
  local copies, waits for them, and re-layouts  19.1 us (14%)
    pallas_call x1, Pallas kernels, local(): pl.pallas_call(functools.partial(kernel, S, C, factor), out_shape=(jax.Sh...  115 us
    reshape x2, local copies, waits for them, and re-layouts, local(): back = filters[::-1].reshape(3, 9, ch, C, ch)  6.58 us
    unnamed x10, local copies, waits for them, and re-layouts  3.87 us

profile of v1, /device:TPU:9, one launch (start us, length us, event | category | flops | bytes accessed | tf_op | source)
XLA Modules:
  0.0 135.2 jit_solution(14280313508004988195)
XLA Ops:
  0.6 0.0 copy-start.3
  0.6 1.3 copy_bitcast_fusion
  1.9 0.1 copy-done.3
  2.0 1.0 rev.3
  3.0 3.0 %reshape.26 = bf16[3,9,64,4,64]{4,3,2,1,0:T(4,128)(2,1)S(1)} reshape(bf16[27,64,256]{2,1,0:T(8,128)(2,1)} %rev.3) | data formatting | bytes 1769472 | tf_op jit(solution)/shard_map/reshape | solution.py:202
  6.0 3.6 %copy.23 = bf16[3,9,64,4,64]{2,4,0,1,3:T(8,128)(2,1)} copy(bf16[3,9,64,4,64]{4,3,2,1,0:T(4,128)(2,1)S(1)} %reshape.26) | data formatting | bytes 1769472 | tf_op jit(solution)/shard_map/reshape | solution.py:202
  9.6 1.9 %copy.25.wt = bf16[4,9,64,192]{3,2,1,0:T(8,128)(2,1)S(1)} copy(bf16[4,9,64,192]{2,3,1,0:T(8,128)(2,1)} %bitcast.17) | data formatting | bytes 1769472 | tf_op jit(solution)/shard_map/reshape | solution.py:203
  11.5 1.0 copy.22
  12.5 1.5 %copy.24.wf = bf16[9,256,192]{2,1,0:T(8,128)(2,1)S(1)} copy(bf16[9,256,192]{1,2,0:T(8,128)(2,1)} %bitcast.19) | data formatting | bytes 1769472 | tf_op jit(solution)/shard_map/reshape | solution.py:201
  14.0 115.4 %shard_map.58 = (bf16[2,64,1536]{2,1,0:T(8,128)(2,1)S(1)}, bf16[2,64,1536]{2,1,0:T(8,128)(2,1)S(1)}, f32[9,32,192]{2,1,0:T(8,128)S(1)}) custom-call(bf16[2,64,1536]{2,1,0:T(8,128)(2,1)S(1)} %get-tuple-element.19.x, bf16[2,64,1536]{2,1,0:T(8,128)(2,1)S(1)} %get-tuple-element.18.g, bf16[9,256,192]{2,1,0:T(8,128)(2,1)S(1)} %copy.24.wf, ...), custom_call_target="tpu_custom_call" | custom-call | tf_op jit(solution)/shard_map/pallas_call | solution.py:206
  129.4 0.0 copy-start
  129.4 0.7 copy-done
  130.2 0.0 copy-start.2
  130.2 0.7 copy-done.2
  130.9 0.0 copy-start.1
  130.9 1.2 reshape.28
  132.1 0.8 copy.26
  132.9 0.0 copy-done.1
  132.9 1.2 copy.27
  134.1 1.1 copy.28
Async XLA Ops:
  0.6 1.4 %copy-start.3 = (bf16[27,64,256]{2,1,0:T(8,128)(2,1)S(1)}, bf16[27,64,256]{2,1,0:T(8,128)(2,1)}, u32[]{:S(2)}) copy-start(bf16[27,64,256]{2,1,0:T(8,128)(2,1)} %param.4) | copy-start | bytes 2654212
  129.4 0.7 copy-start
  130.2 0.7 copy-start.2
  130.9 2.0 %copy-start.1 = (bf16[2,64,1536]{2,1,0:T(8,128)(2,1)S(1)}, bf16[2,64,1536]{2,1,0:T(8,128)(2,1)}, u32[]{:S(2)}) copy-start(bf16[2,64,1536]{2,1,0:T(8,128)(2,1)} %copy-done) | copy-start | bytes 1179652

commit v2 on v1

v2 whole, which is shorter than its diff:
```python
import functools
import math

import jax
import jax.numpy as jnp
from jax import lax
from jax.experimental import pallas as pl
from jax.experimental.pallas import tpu as pltpu
from jax.sharding import PartitionSpec as P

W = 64
MESH = pl.DeviceIdType.MESH
F32 = jnp.float32
BF16 = jnp.bfloat16


def turn_and_shift(src, dst, s):
    cells = src.shape[2]

    def step(m, carry):
        turned = src[s, :, pl.ds(pl.multiple_of(m * 128, 128), 128)].astype(F32).T
        for h in range(128 // W):
            row = turned[h * W : (h + 1) * W]
            at = pl.ds(pl.multiple_of(m * 128 + (h + 1) * W, W), W)
            dst[0, s, at, :] = pltpu.roll(row, 1, 0).astype(BF16)
            dst[1, s, at, :] = row.astype(BF16)
            dst[2, s, at, :] = pltpu.roll(row, W - 1, 0).astype(BF16)
        return carry

    lax.fori_loop(0, cells // 128, step, 0)
    for r in range(3):
        dst[r, s, 0:W, :] = dst[r, s, cells : cells + W, :]
        dst[r, s, cells + W : cells + 2 * W, :] = dst[r, s, W : 2 * W, :]


def conv(src, weights, y, s):
    cells = y.shape[2]
    chunk = 512

    def step(n, carry):
        total = None
        for q in range(3):
            for r in range(3):
                part = jnp.dot(
                    src[r, s, pl.ds(pl.multiple_of(n * chunk + q * W, W), chunk), :],
                    weights[3 * q + r],
                    preferred_element_type=F32,
                )
                total = part if total is None else total + part
        y[s, :, pl.ds(pl.multiple_of(n * chunk, chunk), chunk)] = total.T
        return carry

    lax.fori_loop(0, cells // chunk, step, 0)


def finish(y, rim, out):
    planes = y.shape[0]
    ch = out.shape[1]
    for d in range(planes):
        total = y[d, ch : 2 * ch, :]
        total = total + (y[d - 1, 0:ch, :] if d > 0 else rim[0])
        total = total + (y[d + 1, 2 * ch : 3 * ch, :] if d < planes - 1 else rim[1])
        out[d] = total.astype(out.dtype)


def group_of(S):
    return next(n for n in (8, 4, 2, 1) if S % n == 0)


def kernel(
    S, C, factor,
    x, g, w,
    feat, igrad, dw,
    xg, gg, wf, wr, wg, xt, gt, yx, yg, g3, grim, xrim, irim, dwt, dwr,
    own_sem, xu_s, xu_r, xd_s, xd_r, gu_s, gu_r, gd_s, gd_r,
    w_s, w_r, v_s, v_r, a_s, a_r, gr_s, gr_r, xr_s, xr_r, ir_s, ir_r, d_s, d_r,
):
    planes, ch, cells = x.shape
    cs = dwt.shape[1] // S
    me_s = lax.axis_index("slab")
    me_c = lax.axis_index("chan")
    group = group_of(S)
    many = 8 // group
    base = lax.div(me_s, group) * group
    place = me_s - base

    barrier = pltpu.get_barrier_semaphore()
    for k in range(1, S):
        pl.semaphore_signal(barrier, inc=1, device_id={"slab": lax.rem(me_s + k, S)}, device_id_type=MESH)
    for k in range(1, C):
        pl.semaphore_signal(barrier, inc=1, device_id={"chan": lax.rem(me_c + k, C)}, device_id_type=MESH)
    pl.semaphore_wait(barrier, S - 1 + C - 1)

    def rows_of(j):
        return pl.ds(pl.multiple_of(j * ch, ch), ch)

    def to_chan(peer, src, dst, send, recv):
        return pltpu.make_async_remote_copy(
            src_ref=src, dst_ref=dst, send_sem=send, recv_sem=recv,
            device_id={"chan": peer}, device_id_type=MESH,
        )

    def to_slab(peer, src, dst, send, recv):
        return pltpu.make_async_remote_copy(
            src_ref=src, dst_ref=dst, send_sem=send, recv_sem=recv,
            device_id={"slab": peer}, device_id_type=MESH,
        )

    right, left = lax.rem(me_s + 1, S), lax.rem(me_s + S - 1, S)

    def low_rim(low, dst, send, recv):
        return to_slab(left, low, dst.at[1], send.at[1], recv.at[1])

    def high_rim(high, dst, send, recv):
        return to_slab(right, high, dst.at[0], send.at[0], recv.at[0])

    class Line:
        def __init__(self, src, dst, us, ur, ds, dr):
            self.src, self.dst, self.sems = src, dst, (us, ur, ds, dr)

        def up(self, s, h):
            rows = rows_of(lax.rem(me_c - (h - 1) + C, C))
            src = self.src.at[s] if h == 1 else self.dst.at[s, rows, :]
            us, ur, _, _ = self.sems
            return to_chan(
                lax.rem(me_c + 1, C), src, self.dst.at[s, rows, :], us.at[s, h - 1], ur.at[s, h - 1]
            )

        def down(self, s, h):
            rows = rows_of(lax.rem(me_c + h - 1, C))
            src = self.src.at[s] if h == 1 else self.dst.at[s, rows, :]
            _, _, ds, dr = self.sems
            return to_chan(
                lax.rem(me_c + C - 1, C), src, self.dst.at[s, rows, :], ds.at[s, h - 1], dr.at[s, h - 1]
            )

        def start(self, s):
            pl.when(me_c < C - 1)(lambda: self.up(s, 1).start())
            pl.when(me_c > 0)(lambda: self.down(s, 1).start())

        def hop(self, s, h):
            pl.when(me_c >= h)(lambda: self.up(s, h).wait_recv())
            if h < C - 1:
                pl.when((me_c >= h) & (me_c < C - 1))(lambda: self.up(s, h + 1).start())
            pl.when(me_c + h <= C - 1)(lambda: self.down(s, h).wait_recv())
            if h < C - 1:
                pl.when((me_c + h <= C - 1) & (me_c > 0))(lambda: self.down(s, h + 1).start())

        def drain(self, s):
            for h in range(1, C):
                pl.when((me_c >= h - 1) & (me_c < C - 1))(lambda h=h: self.up(s, h).wait_send())
                pl.when((me_c + h - 1 <= C - 1) & (me_c > 0))(lambda h=h: self.down(s, h).wait_send())

    xl = Line(x, xg, xu_s, xu_r, xd_s, xd_r)
    gl = Line(g, gg, gu_s, gu_r, gd_s, gd_r)
    mine = rows_of(me_c)
    hops = [(h, s) for h in range(1, C) for s in range(planes)]

    for s in range(planes):
        xl.start(s)
    g_rims = [
        low_rim(g.at[0], grim, gr_s, gr_r),
        high_rim(g.at[planes - 1], grim, gr_s, gr_r),
    ]
    for c in g_rims:
        c.start()
    own = [
        pltpu.make_async_copy(x, xg.at[:, mine, :], own_sem.at[0]),
        pltpu.make_async_copy(g, gg.at[:, mine, :], own_sem.at[1]),
    ]
    for c in own:
        c.start()

    def turn_weights(t, carry):
        both = jnp.concatenate([w[t], w[9 + t], w[18 + t]], axis=0)
        wf[t] = both.astype(F32).T.astype(BF16)
        return carry

    lax.fori_loop(0, 9, turn_weights, 0)
    block = pl.ds(place * many, many)
    w_copies = []
    for k in range(1, C):
        peer = lax.rem(me_c + k, C)
        w_copies += [
            to_chan(peer, wf.at[block, rows_of(peer), :], wr.at[me_c, block], w_s.at[k - 1], w_r.at[k - 1]),
            to_chan(peer, wf.at[8, rows_of(peer), :], wr.at[me_c, 8], v_s.at[k - 1], v_r.at[k - 1]),
        ]
    for c in w_copies:
        c.start()
    own_w = [
        pltpu.make_async_copy(wf.at[block, mine, :], wr.at[me_c, block], own_sem.at[2]),
        pltpu.make_async_copy(wf.at[8, mine, :], wr.at[me_c, 8], own_sem.at[3]),
    ]
    for c in own_w:
        c.start()
    for c in own + own_w:
        c.wait()
    waiting = list(hops)
    for _ in range(min(planes, len(waiting) - planes)):
        h, s = waiting.pop(0)
        xl.hop(s, h)
    for c in w_copies:
        c.wait()
    a_copies = [
        to_slab(
            base + lax.rem(place + k, group),
            wr.at[:, block], wr.at[:, block], a_s.at[k - 1], a_r.at[k - 1],
        )
        for k in range(1, group)
    ]
    for c in a_copies:
        c.start()
    for c in g_rims:
        c.wait()
    for s in range(planes):
        for p in range(3):
            d = s - (p - 1)
            plane = grim[0] if d < 0 else grim[1] if d >= planes else g[d]
            g3[s, p * ch : (p + 1) * ch, :] = plane
    while len(waiting) > planes:
        h, s = waiting.pop(0)
        xl.hop(s, h)
    for c in a_copies:
        c.wait()

    def place_weights(t, carry):
        for z in range(C):
            turned = wr[z, t].astype(F32).T
            parts = [turned[p * ch : (p + 1) * ch] for p in (2, 1, 0)]
            wg[8 - t, z * ch : (z + 1) * ch, :] = jnp.concatenate(parts, axis=1).astype(BF16)
        return carry

    lax.fori_loop(0, 9, place_weights, 0)

    for s in range(planes):
        h, _ = waiting.pop(0)
        xl.hop(s, h)
        if s == 0:
            for d in range(planes):
                gl.start(d)
        turn_and_shift(xg, xt, s)

    def weight_step(t, carry):
        total = None
        for s in range(planes):
            part = jnp.dot(
                g3[s],
                xt[lax.rem(t, 3), s, pl.ds(pl.multiple_of(lax.div(t, 3) * W, W), cells), :],
                preferred_element_type=F32,
            )
            total = part if total is None else total + part
        dwt[t] = total.T
        return carry

    waiting = list(hops)

    def next_hop():
        if len(waiting) > planes:
            h, s = waiting.pop(0)
            gl.hop(s, h)

    next_hop()
    for q in range(3):
        lax.fori_loop(3 * q, 3 * q + 3, weight_step, 0)
        next_hop()
    d_copies = []
    for k in range(1, S):
        peer = lax.rem(me_s + k, S)
        d_copies.append(
            to_slab(
                peer, dwt.at[:, pl.ds(pl.multiple_of(peer * cs, cs), cs), :],
                dwr.at[k - 1], d_s.at[k - 1], d_r.at[k - 1],
            )
        )
    for c in d_copies:
        c.start()
    x_rims = [
        low_rim(yx.at[0, 2 * ch : 3 * ch, :], xrim, xr_s, xr_r),
        high_rim(yx.at[planes - 1, 0:ch, :], xrim, xr_s, xr_r),
    ]
    for s in range(planes):
        conv(xt, wf, yx, s)
        if s == 0:
            x_rims[0].start()
        if s == planes - 1:
            x_rims[1].start()
        next_hop()
    while len(waiting) > planes:
        next_hop()
    i_rims = [
        low_rim(yg.at[0, 2 * ch : 3 * ch, :], irim, ir_s, ir_r),
        high_rim(yg.at[planes - 1, 0:ch, :], irim, ir_s, ir_r),
    ]
    for s in range(planes):
        h, _ = waiting.pop(0)
        gl.hop(s, h)
        turn_and_shift(gg, gt, s)
        conv(gt, wg, yg, s)
        if s == 0:
            i_rims[0].start()
        if s == planes - 1:
            i_rims[1].start()
    for c in x_rims:
        c.wait()
    finish(yx, xrim, feat)
    for c in d_copies:
        c.wait()
    total = dwt[:, pl.ds(pl.multiple_of(me_s * cs, cs), cs), :]
    for k in range(S - 1):
        total = total + dwr[k]
    total = total * factor
    for p in range(3):
        dw[9 * p : 9 * p + 9] = total[:, :, p * ch : (p + 1) * ch]
    for s in range(planes):
        xl.drain(s)
        gl.drain(s)
    for c in i_rims:
        c.wait()
    finish(yg, irim, igrad)


def local(inputs, filters, cotangent):
    S = lax.axis_size("slab")
    C = lax.axis_size("chan")
    ch, planes, cells = inputs.shape
    wide = C * ch
    cs = wide // S
    group = group_of(S)
    factor = 1.0 / math.sqrt(planes * S * cells)
    x = inputs.transpose(1, 0, 2)
    g = cotangent.transpose(1, 0, 2)
    dma = pltpu.SemaphoreType.DMA
    vmem = pl.BlockSpec(memory_space=pltpu.VMEM)
    feat, igrad, dw = pl.pallas_call(
        functools.partial(kernel, S, C, factor),
        out_shape=(
            jax.ShapeDtypeStruct((planes, ch, cells), BF16),
            jax.ShapeDtypeStruct((planes, ch, cells), BF16),
            jax.ShapeDtypeStruct((27, cs, ch), F32),
        ),
        in_specs=[vmem] * 3,
        out_specs=[vmem] * 3,
        scratch_shapes=[
            pltpu.VMEM((planes, wide, cells), BF16),
            pltpu.VMEM((planes, wide, cells), BF16),
            pltpu.VMEM((9, wide, 3 * ch), BF16),
            pltpu.VMEM((C, 9, ch, 3 * ch), BF16),
            pltpu.VMEM((9, wide, 3 * ch), BF16),
            pltpu.VMEM((3, planes, cells + 2 * W, wide), BF16),
            pltpu.VMEM((3, planes, cells + 2 * W, wide), BF16),
            pltpu.VMEM((planes, 3 * ch, cells), F32),
            pltpu.VMEM((planes, 3 * ch, cells), F32),
            pltpu.VMEM((planes, 3 * ch, cells), BF16),
            pltpu.VMEM((2, ch, cells), BF16),
            pltpu.VMEM((2, ch, cells), F32),
            pltpu.VMEM((2, ch, cells), F32),
            pltpu.VMEM((9, wide, 3 * ch), F32),
            pltpu.VMEM((S - 1, 9, cs, 3 * ch), F32),
            dma((4,)),
        ]
        + [dma((planes, C - 1))] * 8
        + [dma((C - 1,))] * 4
        + [dma((max(group - 1, 1),))] * 2
        + [dma((2,))] * 6
        + [dma((S - 1,))] * 2,
        compiler_params=pltpu.CompilerParams(
            collective_id=0, has_side_effects=True, vmem_limit_bytes=48 * 1024 * 1024
        ),
    )(x, g, filters)
    return (feat.transpose(1, 0, 2), igrad.transpose(1, 0, 2), dw.transpose(0, 2, 1))


def solution(mesh):
    placed = (P("chan", "slab", None), P(None, "chan", None), P("chan", "slab", None))
    return jax.shard_map(
        local,
        mesh=mesh,
        in_specs=placed,
        out_specs=(P("chan", "slab", None), P("chan", "slab", None), P(None, "chan", "slab")),
        check_vma=False,
    )
```

time: 135 us -> 105 us (0.78)
  the two profiles are of different devices: /device:TPU:9 before, /device:TPU:0 now
where the time goes in v2:
time: 105 us
  Pallas kernels  99.8 us (95%)
  local copies, waits for them, and re-layouts  4.45 us (4%)
    pallas_call x1, Pallas kernels, local(): pl.pallas_call(functools.partial(kernel, S, C, factor), out_shape=(jax.Sh...  99.8 us
    unnamed x5, local copies, waits for them, and re-layouts  3.17 us

profile of v2, /device:TPU:0, one launch (start us, length us, event | category | flops | bytes accessed | tf_op | source)
XLA Modules:
  0.0 104.9 jit_solution(6164295863206156676)
XLA Ops:
  0.6 0.0 copy-start
  0.6 1.3 %copy_bitcast_fusion = (bf16[2,64,1536]{2,1,0:T(8,128)(2,1)S(1)}, bf16[2,64,1536]{2,1,0:T(8,128)(2,1)S(1)}) fusion(bf16[64,2,1536]{2,1,0:T(2,128)(2,1)} %param.5, bf16[64,2,1536]{2,1,0:T(2,128)(2,1)} %param.3), kind=kLoop, calls=%fused_computation | loop fusion | bytes 1572864 | tf_op jit(solution)/shard_map/transpose | solution.py:331
  1.9 0.1 copy-done
  2.0 99.8 %shard_map.58 = (bf16[2,64,1536]{2,1,0:T(8,128)(2,1)S(1)}, bf16[2,64,1536]{2,1,0:T(8,128)(2,1)S(1)}, f32[27,32,64]{2,1,0:T(8,128)S(1)}) custom-call(bf16[2,64,1536]{2,1,0:T(8,128)(2,1)S(1)} %get-tuple-element.13.x, bf16[2,64,1536]{2,1,0:T(8,128)(2,1)S(1)} %get-tuple-element.12.g, bf16[27,64,256]{2,1,0:T(8,128)(2,1)S(1)} %copy-done), custom_call_target="tpu_custom_call" | custom-call | tf_op jit(solution)/shard_map/pallas_call | solution.py:334
  101.9 1.2 %copy.8 = bf16[64,2,1536]{2,1,0:T(2,128)(2,1)} copy(bf16[64,2,1536]{2,0,1:T(8,128)(2,1)S(1)} %bitcast.9) | data formatting | bytes 786432
  103.0 1.1 %copy.9 = bf16[64,2,1536]{2,1,0:T(2,128)(2,1)} copy(bf16[64,2,1536]{2,0,1:T(8,128)(2,1)S(1)} %bitcast.8) | data formatting | bytes 786432
  104.2 0.8 copy.13
Async XLA Ops:
  0.6 1.4 %copy-start = (bf16[27,64,256]{2,1,0:T(8,128)(2,1)S(1)}, bf16[27,64,256]{2,1,0:T(8,128)(2,1)}, u32[]{:S(2)}) copy-start(bf16[27,64,256]{2,1,0:T(8,128)(2,1)} %w.1) | copy-start | bytes 2654212

commit v3 on v2

v3 whole, which is shorter than its diff:
```python
import functools
import math

import jax
import jax.numpy as jnp
from jax import lax
from jax.experimental import pallas as pl
from jax.experimental.pallas import tpu as pltpu
from jax.sharding import PartitionSpec as P

W = 64
CHUNK = 512
MESH = pl.DeviceIdType.MESH
F32 = jnp.float32
BF16 = jnp.bfloat16


def turn_and_shift(src, dst, s):
    cells = src.shape[2]

    def step(m, carry):
        turned = src[s, :, pl.ds(pl.multiple_of(m * 128, 128), 128)].astype(F32).T
        for h in range(128 // W):
            row = turned[h * W : (h + 1) * W]
            at = pl.ds(pl.multiple_of(m * 128 + (h + 1) * W, W), W)
            dst[0, s, at, :] = pltpu.roll(row, 1, 0).astype(BF16)
            dst[1, s, at, :] = row.astype(BF16)
            dst[2, s, at, :] = pltpu.roll(row, W - 1, 0).astype(BF16)
        return carry

    lax.fori_loop(0, cells // 128, step, 0)
    for r in range(3):
        dst[r, s, 0:W, :] = dst[r, s, cells : cells + W, :]
        dst[r, s, cells + W : cells + 2 * W, :] = dst[r, s, W : 2 * W, :]


def conv(src, weights, partial, y, s, after):
    planes = weights.shape[0]
    cells = partial.shape[0]
    chunk = CHUNK

    def step(n, carry):
        here = pl.ds(pl.multiple_of(n * chunk, chunk), chunk)
        total = None if s == 0 else partial[here, :]
        for q in range(3):
            for r in range(3):
                part = jnp.dot(
                    src[r, s, pl.ds(pl.multiple_of(n * chunk + q * W, W), chunk), :],
                    weights[s, 3 * q + r],
                    preferred_element_type=F32,
                )
                total = part if total is None else total + part
        if s < planes - 1:
            partial[here, :] = total
        else:
            y[:, here] = total.T
            after(n)
        return carry

    lax.fori_loop(0, cells // chunk, step, 0)


def finish(y, rim, out, n):
    planes, ch, _ = out.shape
    here = slice(n * CHUNK, (n + 1) * CHUNK)
    for d in range(planes):
        total = y[(d + 1) * ch : (d + 2) * ch, here]
        if d == 0:
            total = total + rim[0, :, here]
        if d == planes - 1:
            total = total + rim[1, :, here]
        out[d, :, here] = total.astype(out.dtype)


def set_apart(blocks, s, planes, axis):
    ch = blocks[0].shape[axis]
    shape = list(blocks[0].shape)
    parts = list(blocks)
    if s > 0:
        shape[axis] = s * ch
        parts = [jnp.zeros(shape, F32)] + parts
    if s < planes - 1:
        shape[axis] = (planes - 1 - s) * ch
        parts = parts + [jnp.zeros(shape, F32)]
    return jnp.concatenate(parts, axis=axis)


def group_of(S):
    return next(n for n in (8, 4, 2, 1) if S % n == 0)


def kernel(
    S, C, factor,
    x, g, w,
    feat, igrad, dw,
    xg, gg, wf, ws, wr, wg, xt, gt, px, pg, yx, yg, g3, grim, xrim, irim, dwa, dwt, dwr,
    own_sem, xu_s, xu_r, xd_s, xd_r, gu_s, gu_r, gd_s, gd_r,
    w_s, w_r, v_s, v_r, a_s, a_r, gr_s, gr_r, xr_s, xr_r, ir_s, ir_r, d_s, d_r,
):
    planes, ch, cells = x.shape
    cs = dwt.shape[1] // S
    me_s = lax.axis_index("slab")
    me_c = lax.axis_index("chan")
    group = group_of(S)
    many = 8 // group
    base = lax.div(me_s, group) * group
    place = me_s - base

    barrier = pltpu.get_barrier_semaphore()
    for k in range(1, S):
        pl.semaphore_signal(barrier, inc=1, device_id={"slab": lax.rem(me_s + k, S)}, device_id_type=MESH)
    for k in range(1, C):
        pl.semaphore_signal(barrier, inc=1, device_id={"chan": lax.rem(me_c + k, C)}, device_id_type=MESH)
    pl.semaphore_wait(barrier, S - 1 + C - 1)

    def rows_of(j):
        return pl.ds(pl.multiple_of(j * ch, ch), ch)

    def to_chan(peer, src, dst, send, recv):
        return pltpu.make_async_remote_copy(
            src_ref=src, dst_ref=dst, send_sem=send, recv_sem=recv,
            device_id={"chan": peer}, device_id_type=MESH,
        )

    def to_slab(peer, src, dst, send, recv):
        return pltpu.make_async_remote_copy(
            src_ref=src, dst_ref=dst, send_sem=send, recv_sem=recv,
            device_id={"slab": peer}, device_id_type=MESH,
        )

    right, left = lax.rem(me_s + 1, S), lax.rem(me_s + S - 1, S)

    class Unit:
        def __init__(self, src, dst, s, us, ur, ds, dr):
            self.src, self.dst, self.s = src, dst, s
            self.sems = ((1, us, ur), (-1, ds, dr))

        def copy(self, way, send, recv, h, origin):
            rows = rows_of(lax.rem(me_c - way * origin + C, C))
            dst = self.dst.at[self.s, rows, :]
            src = self.src.at[self.s] if origin == 0 else dst
            peer = lax.rem(me_c + way * (h - origin) + C, C)
            return to_chan(peer, src, dst, send.at[self.s, h - 1], recv.at[self.s, h - 1])

        def sends(self, act, origin):
            for h in (origin + 2, origin + 1):
                if h > C - 1:
                    continue
                for way, send, recv in self.sems:
                    first, last = me_c - way * origin, me_c + way * (h - origin)
                    ok = (first >= 0) & (first <= C - 1) & (last >= 0) & (last <= C - 1)
                    pl.when(ok)(lambda c=self.copy(way, send, recv, h, origin): act(c))

        def take(self, h):
            for way, send, recv in self.sems:
                first = me_c - way * h
                pl.when((first >= 0) & (first <= C - 1))(
                    lambda c=self.copy(way, send, recv, h, h): c.wait_recv()
                )

        def start(self):
            self.sends(lambda c: c.start(), 0)

        def relay(self):
            for h in range(2, C - 1, 2):
                self.take(h)
                self.sends(lambda c: c.start(), h)

        def rest(self):
            for h in range(1, C):
                if h % 2 == 1 or h >= C - 1:
                    self.take(h)

        def drain(self):
            for origin in range(0, C - 1, 2):
                self.sends(lambda c: c.wait_send(), origin)

    xu = [Unit(x, xg, s, xu_s, xu_r, xd_s, xd_r) for s in range(planes)]
    gu = [Unit(g, gg, s, gu_s, gu_r, gd_s, gd_r) for s in range(planes)]
    units = xu + gu
    mine = rows_of(me_c)

    units[0].start()
    g_rims = [
        to_slab(left, g.at[0], grim.at[1], gr_s.at[1], gr_r.at[1]),
        to_slab(right, g.at[planes - 1], grim.at[0], gr_s.at[0], gr_r.at[0]),
    ]
    for c in g_rims:
        c.start()
    own = [
        pltpu.make_async_copy(x, xg.at[:, mine, :], own_sem.at[0]),
        pltpu.make_async_copy(g, gg.at[:, mine, :], own_sem.at[1]),
    ]
    for c in own:
        c.start()

    def turn_weights(t, carry):
        blocks = [w[18 + t].astype(F32), w[9 + t].astype(F32), w[t].astype(F32)]
        for s in range(planes):
            turned = set_apart(blocks, s, planes, 0).T.astype(BF16)
            wf[s, t] = turned
            if s == 0:
                ws[t] = turned[:, : 3 * ch]
        return carry

    lax.fori_loop(0, 9, turn_weights, 0)
    units[0].relay()
    units[1].start()
    block = pl.ds(place * many, many)
    w_copies = []
    for k in range(1, C):
        peer = lax.rem(me_c + k, C)
        w_copies += [
            to_chan(peer, ws.at[block, rows_of(peer), :], wr.at[me_c, block], w_s.at[k - 1], w_r.at[k - 1]),
            to_chan(peer, ws.at[8, rows_of(peer), :], wr.at[me_c, 8], v_s.at[k - 1], v_r.at[k - 1]),
        ]
    for c in w_copies:
        c.start()
    own += [
        pltpu.make_async_copy(ws.at[block, mine, :], wr.at[me_c, block], own_sem.at[2]),
        pltpu.make_async_copy(ws.at[8, mine, :], wr.at[me_c, 8], own_sem.at[3]),
    ]
    for c in own[2:]:
        c.start()
    for c in own:
        c.wait()
    for c in g_rims:
        c.wait()
    for s in range(planes):
        for p in range(3):
            d = s - (p - 1)
            plane = grim[0] if d < 0 else grim[1] if d >= planes else g[d]
            g3[s, p * ch : (p + 1) * ch, :] = plane

    def weight_step(s, t, carry):
        total = jnp.dot(
            g3[s],
            xt[lax.rem(t, 3), s, pl.ds(pl.multiple_of(lax.div(t, 3) * W, W), cells), :],
            preferred_element_type=F32,
        )
        if s > 0:
            total = total + dwa[t]
        if s < planes - 1:
            dwa[t] = total
        else:
            dwt[t] = total.T
        return carry

    def x_rim(n):
        return rim_copies(yx, xrim, xr_s, xr_r, n)

    def i_rim(n):
        return rim_copies(yg, irim, ir_s, ir_r, n)

    def rim_copies(y, rim, send, recv, n):
        here = pl.ds(n * CHUNK if isinstance(n, int) else pl.multiple_of(n * CHUNK, CHUNK), CHUNK)
        return [
            to_slab(left, y.at[0:ch, here], rim.at[1, :, here], send.at[1, n], recv.at[1, n]),
            to_slab(
                right, y.at[(planes + 1) * ch : (planes + 2) * ch, here], rim.at[0, :, here],
                send.at[0, n], recv.at[0, n],
            ),
        ]

    def start_all(copies):
        for c in copies:
            c.start()

    a_copies = [
        to_slab(
            base + lax.rem(place + k, group),
            wr.at[:, block], wr.at[:, block], a_s.at[k - 1], a_r.at[k - 1],
        )
        for k in range(1, group)
    ]
    d_copies = []
    for k in range(1, S):
        peer = lax.rem(me_s + k, S)
        d_copies.append(
            to_slab(
                peer, dwt.at[:, pl.ds(pl.multiple_of(peer * cs, cs), cs), :],
                dwr.at[k - 1], d_s.at[k - 1], d_r.at[k - 1],
            )
        )

    def place_weights(t, carry):
        for z in range(C):
            turned = wr[z, t].astype(F32).T
            parts = [turned[p * ch : (p + 1) * ch] for p in (2, 1, 0)]
            for s in range(planes):
                wg[s, 8 - t, z * ch : (z + 1) * ch, :] = set_apart(parts, s, planes, 1).astype(BF16)
        return carry

    def go_on(i):
        if i < len(units):
            units[i].relay()
        if i + 1 < len(units):
            units[i + 1].start()

    for s in range(planes):
        units[s].rest()
        turn_and_shift(xg, xt, s)
        lax.fori_loop(0, 9, functools.partial(weight_step, s), 0)
        if s == planes - 1:
            start_all(d_copies)
        go_on(s + 1)
        conv(xt, wf, px, yx, s, lambda n: start_all(x_rim(n)))
        if s == 0:
            for c in w_copies:
                c.wait()
            start_all(a_copies)
    for c in a_copies:
        c.wait()
    lax.fori_loop(0, 9, place_weights, 0)
    chunks = cells // CHUNK
    for s in range(planes):
        units[planes + s].rest()
        turn_and_shift(gg, gt, s)
        go_on(planes + s + 1)
        conv(gt, wg, pg, yg, s, lambda n: start_all(i_rim(n)))
        if s == 0:
            for n in range(chunks):
                for c in x_rim(n):
                    c.wait()
                finish(yx, xrim, feat, n)
            for c in d_copies:
                c.wait()
            total = dwt[:, pl.ds(pl.multiple_of(me_s * cs, cs), cs), :]
            for k in range(S - 1):
                total = total + dwr[k]
            total = total * factor
            for p in range(3):
                dw[9 * p : 9 * p + 9] = total[:, :, p * ch : (p + 1) * ch]
    for u in units:
        u.drain()
    for n in range(chunks):
        for c in i_rim(n):
            c.wait()
        finish(yg, irim, igrad, n)


def local(inputs, filters, cotangent):
    S = lax.axis_size("slab")
    C = lax.axis_size("chan")
    ch, planes, cells = inputs.shape
    wide = C * ch
    cs = wide // S
    group = group_of(S)
    spread = (planes + 2) * ch
    factor = 1.0 / math.sqrt(planes * S * cells)
    x = inputs.transpose(1, 0, 2)
    g = cotangent.transpose(1, 0, 2)
    dma = pltpu.SemaphoreType.DMA
    vmem = pl.BlockSpec(memory_space=pltpu.VMEM)
    feat, igrad, dw = pl.pallas_call(
        functools.partial(kernel, S, C, factor),
        out_shape=(
            jax.ShapeDtypeStruct((planes, ch, cells), BF16),
            jax.ShapeDtypeStruct((planes, ch, cells), BF16),
            jax.ShapeDtypeStruct((27, cs, ch), F32),
        ),
        in_specs=[vmem] * 3,
        out_specs=[vmem] * 3,
        scratch_shapes=[
            pltpu.VMEM((planes, wide, cells), BF16),
            pltpu.VMEM((planes, wide, cells), BF16),
            pltpu.VMEM((planes, 9, wide, spread), BF16),
            pltpu.VMEM((9, wide, 3 * ch), BF16),
            pltpu.VMEM((C, 9, ch, 3 * ch), BF16),
            pltpu.VMEM((planes, 9, wide, spread), BF16),
            pltpu.VMEM((3, planes, cells + 2 * W, wide), BF16),
            pltpu.VMEM((3, planes, cells + 2 * W, wide), BF16),
            pltpu.VMEM((cells, spread), F32),
            pltpu.VMEM((cells, spread), F32),
            pltpu.VMEM((spread, cells), F32),
            pltpu.VMEM((spread, cells), F32),
            pltpu.VMEM((planes, 3 * ch, cells), BF16),
            pltpu.VMEM((2, ch, cells), BF16),
            pltpu.VMEM((2, ch, cells), F32),
            pltpu.VMEM((2, ch, cells), F32),
            pltpu.VMEM((9, 3 * ch, wide), F32),
            pltpu.VMEM((9, wide, 3 * ch), F32),
            pltpu.VMEM((S - 1, 9, cs, 3 * ch), F32),
            dma((4,)),
        ]
        + [dma((planes, C - 1))] * 8
        + [dma((C - 1,))] * 4
        + [dma((max(group - 1, 1),))] * 2
        + [dma((2,))] * 2
        + [dma((2, cells // CHUNK))] * 4
        + [dma((S - 1,))] * 2,
        compiler_params=pltpu.CompilerParams(
            collective_id=0, has_side_effects=True, vmem_limit_bytes=48 * 1024 * 1024
        ),
    )(x, g, filters)
    return (feat.transpose(1, 0, 2), igrad.transpose(1, 0, 2), dw.transpose(0, 2, 1))


def solution(mesh):
    placed = (P("chan", "slab", None), P(None, "chan", None), P("chan", "slab", None))
    return jax.shard_map(
        local,
        mesh=mesh,
        in_specs=placed,
        out_specs=(P("chan", "slab", None), P("chan", "slab", None), P(None, "chan", "slab")),
        check_vma=False,
    )
```

time: 105 us -> 106 us (level)
  Pallas kernels: 99.8 us -> 101 us
where the time goes in v3:
time: 106 us
  Pallas kernels  101 us (95%)
  local copies, waits for them, and re-layouts  4.45 us (4%)
    pallas_call x1, Pallas kernels, local(): pl.pallas_call(functools.partial(kernel, S, C, factor), out_shape=(jax.Sh...  101 us
    unnamed x5, local copies, waits for them, and re-layouts  3.17 us

profile of v3, /device:TPU:0, one launch (start us, length us, event | category | flops | bytes accessed | tf_op | source)
XLA Modules:
  0.0 105.8 jit_solution(13509364960468739822)
XLA Ops:
  0.6 0.0 copy-start
  0.6 1.3 %copy_bitcast_fusion = (bf16[2,64,1536]{2,1,0:T(8,128)(2,1)S(1)}, bf16[2,64,1536]{2,1,0:T(8,128)(2,1)S(1)}) fusion(bf16[64,2,1536]{2,1,0:T(2,128)(2,1)} %param.5, bf16[64,2,1536]{2,1,0:T(2,128)(2,1)} %param.3), kind=kLoop, calls=%fused_computation | loop fusion | bytes 1572864 | tf_op jit(solution)/shard_map/transpose | solution.py:352
  1.9 0.1 copy-done
  2.0 100.7 %shard_map.58 = (bf16[2,64,1536]{2,1,0:T(8,128)(2,1)S(1)}, bf16[2,64,1536]{2,1,0:T(8,128)(2,1)S(1)}, f32[27,32,64]{2,1,0:T(8,128)S(1)}) custom-call(bf16[2,64,1536]{2,1,0:T(8,128)(2,1)S(1)} %get-tuple-element.13.x, bf16[2,64,1536]{2,1,0:T(8,128)(2,1)S(1)} %get-tuple-element.12.g, bf16[27,64,256]{2,1,0:T(8,128)(2,1)S(1)} %copy-done), custom_call_target="tpu_custom_call" | custom-call | tf_op jit(solution)/shard_map/pallas_call | solution.py:355
  102.7 1.2 %copy.8 = bf16[64,2,1536]{2,1,0:T(2,128)(2,1)} copy(bf16[64,2,1536]{2,0,1:T(8,128)(2,1)S(1)} %bitcast.9) | data formatting | bytes 786432
  103.8 1.1 %copy.9 = bf16[64,2,1536]{2,1,0:T(2,128)(2,1)} copy(bf16[64,2,1536]{2,0,1:T(8,128)(2,1)S(1)} %bitcast.8) | data formatting | bytes 786432
  105.0 0.8 copy.13
Async XLA Ops:
  0.6 1.4 %copy-start = (bf16[27,64,256]{2,1,0:T(8,128)(2,1)S(1)}, bf16[27,64,256]{2,1,0:T(8,128)(2,1)}, u32[]{:S(2)}) copy-start(bf16[27,64,256]{2,1,0:T(8,128)(2,1)} %w.1) | copy-start | bytes 2654212

commit v4 on v3

--- a/solution.py
+++ b/solution.py
@@ -19,7 +19,7 @@
     cells = src.shape[2]
 
     def step(m, carry):
-        turned = src[s, :, pl.ds(pl.multiple_of(m * 128, 128), 128)].astype(F32).T
+        turned = src[s, :, pl.ds(pl.multiple_of(m * 128, 128), 128)].T.astype(F32)
         for h in range(128 // W):
             row = turned[h * W : (h + 1) * W]
             at = pl.ds(pl.multiple_of(m * 128 + (h + 1) * W, W), W)
@@ -28,7 +28,7 @@
             dst[2, s, at, :] = pltpu.roll(row, W - 1, 0).astype(BF16)
         return carry
 
-    lax.fori_loop(0, cells // 128, step, 0)
+    lax.fori_loop(0, cells // 128, step, 0, unroll=4)
     for r in range(3):
         dst[r, s, 0:W, :] = dst[r, s, cells : cells + W, :]
         dst[r, s, cells + W : cells + 2 * W, :] = dst[r, s, W : 2 * W, :]
@@ -72,17 +72,10 @@
         out[d, :, here] = total.astype(out.dtype)
 
 
-def set_apart(blocks, s, planes, axis):
-    ch = blocks[0].shape[axis]
-    shape = list(blocks[0].shape)
-    parts = list(blocks)
-    if s > 0:
-        shape[axis] = s * ch
-        parts = [jnp.zeros(shape, F32)] + parts
-    if s < planes - 1:
-        shape[axis] = (planes - 1 - s) * ch
-        parts = parts + [jnp.zeros(shape, F32)]
-    return jnp.concatenate(parts, axis=axis)
+def moved(v, by):
+    if by == 0:
+        return v
+    return jnp.concatenate([v[:, v.shape[1] - by :], v[:, : v.shape[1] - by]], axis=1)
 
 
 def group_of(S):
@@ -93,7 +86,7 @@
     S, C, factor,
     x, g, w,
     feat, igrad, dw,
-    xg, gg, wf, ws, wr, wg, xt, gt, px, pg, yx, yg, g3, grim, xrim, irim, dwa, dwt, dwr,
+    xg, gg, wf, we, wg, xt, gt, px, pg, yx, yg, g3, grim, xrim, irim, dwa, dwt, dwr,
     own_sem, xu_s, xu_r, xd_s, xd_r, gu_s, gu_r, gd_s, gd_r,
     w_s, w_r, v_s, v_r, a_s, a_r, gr_s, gr_r, xr_s, xr_r, ir_s, ir_r, d_s, d_r,
 ):
@@ -194,34 +187,45 @@
     for c in own:
         c.start()
 
-    def turn_weights(t, carry):
-        blocks = [w[18 + t].astype(F32), w[9 + t].astype(F32), w[t].astype(F32)]
-        for s in range(planes):
-            turned = set_apart(blocks, s, planes, 0).T.astype(BF16)
-            wf[s, t] = turned
-            if s == 0:
-                ws[t] = turned[:, : 3 * ch]
-        return carry
-
-    lax.fori_loop(0, 9, turn_weights, 0)
-    units[0].relay()
-    units[1].start()
+    blank = [jnp.zeros((ch, (planes - 1) * ch), F32)] if planes > 1 else []
+
+    def split_weights(t, carry):
+        taps = [w[9 * p + t].astype(F32) for p in range(3)]
+        for z in range(C):
+            parts = [tap[:, z * ch : (z + 1) * ch] for tap in taps] + blank
+            we[z, 8 - t] = jnp.concatenate(parts, axis=1).astype(BF16)
+        return carry
+
+    lax.fori_loop(0, 9, split_weights, 0)
     block = pl.ds(place * many, many)
     w_copies = []
     for k in range(1, C):
         peer = lax.rem(me_c + k, C)
         w_copies += [
-            to_chan(peer, ws.at[block, rows_of(peer), :], wr.at[me_c, block], w_s.at[k - 1], w_r.at[k - 1]),
-            to_chan(peer, ws.at[8, rows_of(peer), :], wr.at[me_c, 8], v_s.at[k - 1], v_r.at[k - 1]),
+            to_chan(peer, we.at[peer, block], wg.at[0, block, mine, :], w_s.at[k - 1], w_r.at[k - 1]),
+            to_chan(peer, we.at[peer, 8], wg.at[0, 8, mine, :], v_s.at[k - 1], v_r.at[k - 1]),
         ]
     for c in w_copies:
         c.start()
     own += [
-        pltpu.make_async_copy(ws.at[block, mine, :], wr.at[me_c, block], own_sem.at[2]),
-        pltpu.make_async_copy(ws.at[8, mine, :], wr.at[me_c, 8], own_sem.at[3]),
+        pltpu.make_async_copy(we.at[me_c, block], wg.at[0, block, mine, :], own_sem.at[2]),
+        pltpu.make_async_copy(we.at[me_c, 8], wg.at[0, 8, mine, :], own_sem.at[3]),
     ]
     for c in own[2:]:
         c.start()
+
+    def turn_weights(t, carry):
+        blocks = [w[9 * p + t].astype(F32) for p in (2, 1, 0)]
+        if planes > 1:
+            blocks.append(jnp.zeros(((planes - 1) * ch, C * ch), F32))
+        turned = jnp.concatenate(blocks, axis=0).T
+        for s in range(planes):
+            wf[s, t] = moved(turned, s * ch).astype(BF16)
+        return carry
+
+    lax.fori_loop(0, 9, turn_weights, 0)
+    units[0].relay()
+    units[1].start()
     for c in own:
         c.wait()
     for c in g_rims:
@@ -231,6 +235,17 @@
             d = s - (p - 1)
             plane = grim[0] if d < 0 else grim[1] if d >= planes else g[d]
             g3[s, p * ch : (p + 1) * ch, :] = plane
+    a_copies = [
+        to_slab(
+            base + lax.rem(place + k, group),
+            wg.at[0, block], wg.at[0, block], a_s.at[k - 1], a_r.at[k - 1],
+        )
+        for k in range(1, group)
+    ]
+    for c in w_copies:
+        c.wait()
+    for c in a_copies:
+        c.start()
 
     def weight_step(s, t, carry):
         total = jnp.dot(
@@ -266,13 +281,6 @@
         for c in copies:
             c.start()
 
-    a_copies = [
-        to_slab(
-            base + lax.rem(place + k, group),
-            wr.at[:, block], wr.at[:, block], a_s.at[k - 1], a_r.at[k - 1],
-        )
-        for k in range(1, group)
-    ]
     d_copies = []
     for k in range(1, S):
         peer = lax.rem(me_s + k, S)
@@ -284,39 +292,37 @@
         )
 
     def place_weights(t, carry):
-        for z in range(C):
-            turned = wr[z, t].astype(F32).T
-            parts = [turned[p * ch : (p + 1) * ch] for p in (2, 1, 0)]
-            for s in range(planes):
-                wg[s, 8 - t, z * ch : (z + 1) * ch, :] = set_apart(parts, s, planes, 1).astype(BF16)
-        return carry
-
-    def go_on(i):
+        v = wg[0, t].astype(F32)
+        for s in range(1, planes):
+            wg[s, t] = moved(v, s * ch).astype(BF16)
+        return carry
+
+    def relay(i):
         if i < len(units):
             units[i].relay()
-        if i + 1 < len(units):
-            units[i + 1].start()
+
+    def rest(i):
+        units[i].rest()
+        if i + 2 < len(units):
+            units[i + 2].start()
 
     for s in range(planes):
-        units[s].rest()
+        rest(s)
         turn_and_shift(xg, xt, s)
         lax.fori_loop(0, 9, functools.partial(weight_step, s), 0)
         if s == planes - 1:
             start_all(d_copies)
-        go_on(s + 1)
+        relay(s + 1)
         conv(xt, wf, px, yx, s, lambda n: start_all(x_rim(n)))
         if s == 0:
-            for c in w_copies:
+            for c in a_copies:
                 c.wait()
-            start_all(a_copies)
-    for c in a_copies:
-        c.wait()
-    lax.fori_loop(0, 9, place_weights, 0)
+            lax.fori_loop(0, 9, place_weights, 0)
     chunks = cells // CHUNK
     for s in range(planes):
-        units[planes + s].rest()
+        rest(planes + s)
         turn_and_shift(gg, gt, s)
-        go_on(planes + s + 1)
+        relay(planes + s + 1)
         conv(gt, wg, pg, yg, s, lambda n: start_all(i_rim(n)))
         if s == 0:
             for n in range(chunks):
@@ -365,8 +371,7 @@
             pltpu.VMEM((planes, wide, cells), BF16),
             pltpu.VMEM((planes, wide, cells), BF16),
             pltpu.VMEM((planes, 9, wide, spread), BF16),
-            pltpu.VMEM((9, wide, 3 * ch), BF16),
-            pltpu.VMEM((C, 9, ch, 3 * ch), BF16),
+            pltpu.VMEM((C, 9, ch, spread), BF16),
             pltpu.VMEM((planes, 9, wide, spread), BF16),
             pltpu.VMEM((3, planes, cells + 2 * W, wide), BF16),
             pltpu.VMEM((3, planes, cells + 2 * W, wide), BF16),

time: 106 us -> 100 us (0.943)
  Pallas kernels: 101 us -> 95.2 us
    pallas_call x1, Pallas kernels: 101 us -> 95.2 us  [local(): pl.pallas_call(functools.partial(kernel, S, C, factor), out_shape=(jax.Sh...]
where the time goes in v4:
time: 100 us
  Pallas kernels  95.2 us (95%)
  local copies, waits for them, and re-layouts  4.45 us (4%)
    pallas_call x1, Pallas kernels, local(): pl.pallas_call(functools.partial(kernel, S, C, factor), out_shape=(jax.Sh...  95.2 us
    unnamed x5, local copies, waits for them, and re-layouts  3.17 us

profile of v4, /device:TPU:0, one launch (start us, length us, event | category | flops | bytes accessed | tf_op | source)
XLA Modules:
  0.0 100.3 jit_solution(10892146674364551500)
XLA Ops:
  0.6 0.0 copy-start
  0.6 1.3 %copy_bitcast_fusion = (bf16[2,64,1536]{2,1,0:T(8,128)(2,1)S(1)}, bf16[2,64,1536]{2,1,0:T(8,128)(2,1)S(1)}) fusion(bf16[64,2,1536]{2,1,0:T(2,128)(2,1)} %param.5, bf16[64,2,1536]{2,1,0:T(2,128)(2,1)} %param.3), kind=kLoop, calls=%fused_computation | loop fusion | bytes 1572864 | tf_op jit(solution)/shard_map/transpose | solution.py:358
  1.9 0.1 copy-done
  2.0 95.2 %shard_map.58 = (bf16[2,64,1536]{2,1,0:T(8,128)(2,1)S(1)}, bf16[2,64,1536]{2,1,0:T(8,128)(2,1)S(1)}, f32[27,32,64]{2,1,0:T(8,128)S(1)}) custom-call(bf16[2,64,1536]{2,1,0:T(8,128)(2,1)S(1)} %get-tuple-element.13.x, bf16[2,64,1536]{2,1,0:T(8,128)(2,1)S(1)} %get-tuple-element.12.g, bf16[27,64,256]{2,1,0:T(8,128)(2,1)S(1)} %copy-done), custom_call_target="tpu_custom_call" | custom-call | tf_op jit(solution)/shard_map/pallas_call | solution.py:361
  97.3 1.2 %copy.8 = bf16[64,2,1536]{2,1,0:T(2,128)(2,1)} copy(bf16[64,2,1536]{2,0,1:T(8,128)(2,1)S(1)} %bitcast.9) | data formatting | bytes 786432
  98.4 1.1 %copy.9 = bf16[64,2,1536]{2,1,0:T(2,128)(2,1)} copy(bf16[64,2,1536]{2,0,1:T(8,128)(2,1)S(1)} %bitcast.8) | data formatting | bytes 786432
  99.6 0.8 copy.13
Async XLA Ops:
  0.6 1.4 %copy-start = (bf16[27,64,256]{2,1,0:T(8,128)(2,1)S(1)}, bf16[27,64,256]{2,1,0:T(8,128)(2,1)}, u32[]{:S(2)}) copy-start(bf16[27,64,256]{2,1,0:T(8,128)(2,1)} %w.1) | copy-start | bytes 2654212

commit v5 on v4

--- a/solution.py
+++ b/solution.py
@@ -36,7 +36,8 @@
 
 def conv(src, weights, partial, y, s, after):
     planes = weights.shape[0]
-    cells = partial.shape[0]
+    cells, spread = partial.shape
+    ch = spread // (planes + 2)
     chunk = CHUNK
 
     def step(n, carry):
@@ -52,9 +53,12 @@
                 total = part if total is None else total + part
         if s < planes - 1:
             partial[here, :] = total
-        else:
-            y[:, here] = total.T
-            after(n)
+        if s == 0:
+            y[0:ch, here] = total[:, : max(ch, min(128, total.shape[1]))].T[0:ch]
+            after[0](n)
+        if s == planes - 1:
+            y[ch:, here] = total.T[ch:]
+            after[1](n)
         return carry
 
     lax.fori_loop(0, cells // chunk, step, 0)
@@ -86,12 +90,12 @@
     S, C, factor,
     x, g, w,
     feat, igrad, dw,
-    xg, gg, wf, we, wg, xt, gt, px, pg, yx, yg, g3, grim, xrim, irim, dwa, dwt, dwr,
+    xg, gg, wf, we, wg, xt, gt, px, pg, yx, yg, g3, grim, xrim, irim, dwa, dwt, dwp, dwq, dwr,
     own_sem, xu_s, xu_r, xd_s, xd_r, gu_s, gu_r, gd_s, gd_r,
     w_s, w_r, v_s, v_r, a_s, a_r, gr_s, gr_r, xr_s, xr_r, ir_s, ir_r, d_s, d_r,
 ):
     planes, ch, cells = x.shape
-    cs = dwt.shape[1] // S
+    cs = dw.shape[1]
     me_s = lax.axis_index("slab")
     me_c = lax.axis_index("chan")
     group = group_of(S)
@@ -258,7 +262,9 @@
         if s < planes - 1:
             dwa[t] = total
         else:
-            dwt[t] = total.T
+            turned = total.T
+            for k in range(S):
+                dwt[k % 2, k // 2, t] = turned[k * cs : (k + 1) * cs]
         return carry
 
     def x_rim(n):
@@ -269,26 +275,30 @@
 
     def rim_copies(y, rim, send, recv, n):
         here = pl.ds(n * CHUNK if isinstance(n, int) else pl.multiple_of(n * CHUNK, CHUNK), CHUNK)
-        return [
-            to_slab(left, y.at[0:ch, here], rim.at[1, :, here], send.at[1, n], recv.at[1, n]),
-            to_slab(
+        return (
+            lambda: to_slab(left, y.at[0:ch, here], rim.at[1, :, here], send.at[1, n], recv.at[1, n]),
+            lambda: to_slab(
                 right, y.at[(planes + 1) * ch : (planes + 2) * ch, here], rim.at[0, :, here],
                 send.at[0, n], recv.at[0, n],
             ),
-        ]
+        )
+
+    def starts(rim):
+        return (lambda n: rim(n)[0]().start()), (lambda n: rim(n)[1]().start())
 
     def start_all(copies):
         for c in copies:
             c.start()
 
+    even = lax.rem(me_s, 2)
+    pair = lax.div(me_s, 2)
+    pairs = S // 2
+    p_copy = to_slab(me_s + 1 - 2 * even, dwt.at[1 - even], dwp, own_sem.at[4], own_sem.at[5])
     d_copies = []
-    for k in range(1, S):
-        peer = lax.rem(me_s + k, S)
+    for k in range(1, pairs):
+        other = lax.rem(pair + k, pairs)
         d_copies.append(
-            to_slab(
-                peer, dwt.at[:, pl.ds(pl.multiple_of(peer * cs, cs), cs), :],
-                dwr.at[k - 1], d_s.at[k - 1], d_r.at[k - 1],
-            )
+            to_slab(2 * other + even, dwq.at[other], dwr.at[k - 1], d_s.at[k - 1], d_r.at[k - 1])
         )
 
     def place_weights(t, carry):
@@ -311,9 +321,14 @@
         turn_and_shift(xg, xt, s)
         lax.fori_loop(0, 9, functools.partial(weight_step, s), 0)
         if s == planes - 1:
+            p_copy.start()
+        relay(s + 1)
+        conv(xt, wf, px, yx, s, starts(x_rim))
+        if s == planes - 1:
+            p_copy.wait()
+            for m in range(pairs):
+                dwq[m] = dwt[even, m] + dwp[m]
             start_all(d_copies)
-        relay(s + 1)
-        conv(xt, wf, px, yx, s, lambda n: start_all(x_rim(n)))
         if s == 0:
             for c in a_copies:
                 c.wait()
@@ -323,16 +338,16 @@
         rest(planes + s)
         turn_and_shift(gg, gt, s)
         relay(planes + s + 1)
-        conv(gt, wg, pg, yg, s, lambda n: start_all(i_rim(n)))
+        conv(gt, wg, pg, yg, s, starts(i_rim))
         if s == 0:
             for n in range(chunks):
                 for c in x_rim(n):
-                    c.wait()
+                    c().wait()
                 finish(yx, xrim, feat, n)
             for c in d_copies:
                 c.wait()
-            total = dwt[:, pl.ds(pl.multiple_of(me_s * cs, cs), cs), :]
-            for k in range(S - 1):
+            total = dwq[pair]
+            for k in range(pairs - 1):
                 total = total + dwr[k]
             total = total * factor
             for p in range(3):
@@ -341,7 +356,7 @@
         u.drain()
     for n in range(chunks):
         for c in i_rim(n):
-            c.wait()
+            c().wait()
         finish(yg, irim, igrad, n)
 
 
@@ -384,16 +399,18 @@
             pltpu.VMEM((2, ch, cells), F32),
             pltpu.VMEM((2, ch, cells), F32),
             pltpu.VMEM((9, 3 * ch, wide), F32),
-            pltpu.VMEM((9, wide, 3 * ch), F32),
-            pltpu.VMEM((S - 1, 9, cs, 3 * ch), F32),
-            dma((4,)),
+            pltpu.VMEM((2, S // 2, 9, cs, 3 * ch), F32),
+            pltpu.VMEM((S // 2, 9, cs, 3 * ch), F32),
+            pltpu.VMEM((S // 2, 9, cs, 3 * ch), F32),
+            pltpu.VMEM((S // 2 - 1, 9, cs, 3 * ch), F32),
+            dma((6,)),
         ]
         + [dma((planes, C - 1))] * 8
         + [dma((C - 1,))] * 4
         + [dma((max(group - 1, 1),))] * 2
         + [dma((2,))] * 2
         + [dma((2, cells // CHUNK))] * 4
-        + [dma((S - 1,))] * 2,
+        + [dma((S // 2 - 1,))] * 2,
         compiler_params=pltpu.CompilerParams(
             collective_id=0, has_side_effects=True, vmem_limit_bytes=48 * 1024 * 1024
         ),

time: 100 us -> 85.7 us (0.86)
  Pallas kernels: 95.2 us -> 80.5 us
    pallas_call x1, Pallas kernels: 95.2 us -> 80.5 us  [local(): pl.pallas_call(functools.partial(kernel, S, C, factor), out_shape=(jax.Sh...]
where the time goes in v5:
time: 85.7 us; the launch traced here: 85.6 us
  Pallas kernels  80.5 us (94%)
  local copies, waits for them, and re-layouts  4.45 us (5%)
    pallas_call x1, Pallas kernels, local(): pl.pallas_call(functools.partial(kernel, S, C, factor), out_shape=(jax.Sh...  80.5 us
    unnamed x5, local copies, waits for them, and re-layouts  3.17 us

profile of v5, /device:TPU:0, one launch (start us, length us, event | category | flops | bytes accessed | tf_op | source)
XLA Modules:
  0.0 85.6 jit_solution(6008161758400267461)
XLA Ops:
  0.6 0.0 copy-start
  0.6 1.3 %copy_bitcast_fusion = (bf16[2,64,1536]{2,1,0:T(8,128)(2,1)S(1)}, bf16[2,64,1536]{2,1,0:T(8,128)(2,1)S(1)}) fusion(bf16[64,2,1536]{2,1,0:T(2,128)(2,1)} %param.5, bf16[64,2,1536]{2,1,0:T(2,128)(2,1)} %param.3), kind=kLoop, calls=%fused_computation | loop fusion | bytes 1572864 | tf_op jit(solution)/shard_map/transpose | solution.py:373
  1.9 0.1 copy-done
  2.0 80.5 %shard_map.58 = (bf16[2,64,1536]{2,1,0:T(8,128)(2,1)S(1)}, bf16[2,64,1536]{2,1,0:T(8,128)(2,1)S(1)}, f32[27,32,64]{2,1,0:T(8,128)S(1)}) custom-call(bf16[2,64,1536]{2,1,0:T(8,128)(2,1)S(1)} %get-tuple-element.13.x, bf16[2,64,1536]{2,1,0:T(8,128)(2,1)S(1)} %get-tuple-element.12.g, bf16[27,64,256]{2,1,0:T(8,128)(2,1)S(1)} %copy-done), custom_call_target="tpu_custom_call" | custom-call | tf_op jit(solution)/shard_map/pallas_call | solution.py:376
  82.5 1.2 %copy.8 = bf16[64,2,1536]{2,1,0:T(2,128)(2,1)} copy(bf16[64,2,1536]{2,0,1:T(8,128)(2,1)S(1)} %bitcast.9) | data formatting | bytes 786432
  83.7 1.1 %copy.9 = bf16[64,2,1536]{2,1,0:T(2,128)(2,1)} copy(bf16[64,2,1536]{2,0,1:T(8,128)(2,1)S(1)} %bitcast.8) | data formatting | bytes 786432
  84.8 0.8 copy.13
Async XLA Ops:
  0.6 1.4 %copy-start = (bf16[27,64,256]{2,1,0:T(8,128)(2,1)S(1)}, bf16[27,64,256]{2,1,0:T(8,128)(2,1)}, u32[]{:S(2)}) copy-start(bf16[27,64,256]{2,1,0:T(8,128)(2,1)} %w.1) | copy-start | bytes 2654212

commit v6 on v5

--- a/solution.py
+++ b/solution.py
@@ -28,7 +28,7 @@
             dst[2, s, at, :] = pltpu.roll(row, W - 1, 0).astype(BF16)
         return carry
 
-    lax.fori_loop(0, cells // 128, step, 0, unroll=4)
+    lax.fori_loop(0, cells // 128, step, 0, unroll=6)
     for r in range(3):
         dst[r, s, 0:W, :] = dst[r, s, cells : cells + W, :]
         dst[r, s, cells + W : cells + 2 * W, :] = dst[r, s, W : 2 * W, :]
@@ -61,7 +61,7 @@
             after[1](n)
         return carry
 
-    lax.fori_loop(0, cells // chunk, step, 0)
+    lax.fori_loop(0, cells // chunk, step, 0, unroll=True)
 
 
 def finish(y, rim, out, n):
@@ -200,7 +200,7 @@
             we[z, 8 - t] = jnp.concatenate(parts, axis=1).astype(BF16)
         return carry
 
-    lax.fori_loop(0, 9, split_weights, 0)
+    lax.fori_loop(0, 9, split_weights, 0, unroll=3)
     block = pl.ds(place * many, many)
     w_copies = []
     for k in range(1, C):
@@ -227,7 +227,7 @@
             wf[s, t] = moved(turned, s * ch).astype(BF16)
         return carry
 
-    lax.fori_loop(0, 9, turn_weights, 0)
+    lax.fori_loop(0, 9, turn_weights, 0, unroll=3)
     units[0].relay()
     units[1].start()
     for c in own:
@@ -319,7 +319,7 @@
     for s in range(planes):
         rest(s)
         turn_and_shift(xg, xt, s)
-        lax.fori_loop(0, 9, functools.partial(weight_step, s), 0)
+        lax.fori_loop(0, 9, functools.partial(weight_step, s), 0, unroll=3)
         if s == planes - 1:
             p_copy.start()
         relay(s + 1)
@@ -332,7 +332,7 @@
         if s == 0:
             for c in a_copies:
                 c.wait()
-            lax.fori_loop(0, 9, place_weights, 0)
+            lax.fori_loop(0, 9, place_weights, 0, unroll=3)
     chunks = cells // CHUNK
     for s in range(planes):
         rest(planes + s)

time: 85.7 us -> 85.6 us (level)
  no operation moved by 1% of the time
where the time goes in v6:
time: 85.6 us; the launch traced here: 85.5 us
  Pallas kernels  80.4 us (94%)
  local copies, waits for them, and re-layouts  4.45 us (5%)
    pallas_call x1, Pallas kernels, local(): pl.pallas_call(functools.partial(kernel, S, C, factor), out_shape=(jax.Sh...  80.4 us
    unnamed x5, local copies, waits for them, and re-layouts  3.17 us

profile of v6, /device:TPU:0, one launch (start us, length us, event | category | flops | bytes accessed | tf_op | source)
XLA Modules:
  0.0 85.5 jit_solution(8311984972210660657)
XLA Ops:
  0.6 0.0 copy-start
  0.6 1.3 %copy_bitcast_fusion = (bf16[2,64,1536]{2,1,0:T(8,128)(2,1)S(1)}, bf16[2,64,1536]{2,1,0:T(8,128)(2,1)S(1)}) fusion(bf16[64,2,1536]{2,1,0:T(2,128)(2,1)} %param.5, bf16[64,2,1536]{2,1,0:T(2,128)(2,1)} %param.3), kind=kLoop, calls=%fused_computation | loop fusion | bytes 1572864 | tf_op jit(solution)/shard_map/transpose | solution.py:373
  1.9 0.1 copy-done
  2.0 80.4 %shard_map.58 = (bf16[2,64,1536]{2,1,0:T(8,128)(2,1)S(1)}, bf16[2,64,1536]{2,1,0:T(8,128)(2,1)S(1)}, f32[27,32,64]{2,1,0:T(8,128)S(1)}) custom-call(bf16[2,64,1536]{2,1,0:T(8,128)(2,1)S(1)} %get-tuple-element.13.x, bf16[2,64,1536]{2,1,0:T(8,128)(2,1)S(1)} %get-tuple-element.12.g, bf16[27,64,256]{2,1,0:T(8,128)(2,1)S(1)} %copy-done), custom_call_target="tpu_custom_call" | custom-call | tf_op jit(solution)/shard_map/pallas_call | solution.py:376
  82.4 1.2 %copy.8 = bf16[64,2,1536]{2,1,0:T(2,128)(2,1)} copy(bf16[64,2,1536]{2,0,1:T(8,128)(2,1)S(1)} %bitcast.9) | data formatting | bytes 786432
  83.6 1.1 %copy.9 = bf16[64,2,1536]{2,1,0:T(2,128)(2,1)} copy(bf16[64,2,1536]{2,0,1:T(8,128)(2,1)S(1)} %bitcast.8) | data formatting | bytes 786432
  84.7 0.8 copy.13
Async XLA Ops:
  0.6 1.4 %copy-start = (bf16[27,64,256]{2,1,0:T(8,128)(2,1)S(1)}, bf16[27,64,256]{2,1,0:T(8,128)(2,1)}, u32[]{:S(2)}) copy-start(bf16[27,64,256]{2,1,0:T(8,128)(2,1)} %w.1) | copy-start | bytes 2654212

commit v7 on v6

--- a/solution.py
+++ b/solution.py
@@ -323,12 +323,12 @@
         if s == planes - 1:
             p_copy.start()
         relay(s + 1)
-        conv(xt, wf, px, yx, s, starts(x_rim))
         if s == planes - 1:
             p_copy.wait()
             for m in range(pairs):
                 dwq[m] = dwt[even, m] + dwp[m]
             start_all(d_copies)
+        conv(xt, wf, px, yx, s, starts(x_rim))
         if s == 0:
             for c in a_copies:
                 c.wait()
@@ -339,19 +339,18 @@
         turn_and_shift(gg, gt, s)
         relay(planes + s + 1)
         conv(gt, wg, pg, yg, s, starts(i_rim))
-        if s == 0:
-            for n in range(chunks):
-                for c in x_rim(n):
-                    c().wait()
-                finish(yx, xrim, feat, n)
-            for c in d_copies:
-                c.wait()
-            total = dwq[pair]
-            for k in range(pairs - 1):
-                total = total + dwr[k]
-            total = total * factor
-            for p in range(3):
-                dw[9 * p : 9 * p + 9] = total[:, :, p * ch : (p + 1) * ch]
+    for n in range(chunks):
+        for c in x_rim(n):
+            c().wait()
+        finish(yx, xrim, feat, n)
+    for c in d_copies:
+        c.wait()
+    total = dwq[pair]
+    for k in range(pairs - 1):
+        total = total + dwr[k]
+    total = total * factor
+    for p in range(3):
+        dw[9 * p : 9 * p + 9] = total[:, :, p * ch : (p + 1) * ch]
     for u in units:
         u.drain()
     for n in range(chunks):

time: 85.6 us -> 84.2 us (0.984)
  the two profiles are of different devices: /device:TPU:0 before, /device:TPU:12 now
where the time goes in v7:
time: 84.2 us; the launch traced here: 84.1 us
  Pallas kernels  79 us (94%)
  local copies, waits for them, and re-layouts  4.45 us (5%)
    pallas_call x1, Pallas kernels, local(): pl.pallas_call(functools.partial(kernel, S, C, factor), out_shape=(jax.Sh...  79 us
    unnamed x5, local copies, waits for them, and re-layouts  3.17 us

profile of v7, /device:TPU:12, one launch (start us, length us, event | category | flops | bytes accessed | tf_op | source)
XLA Modules:
  0.0 84.1 jit_solution(18072168519548483744)
XLA Ops:
  0.6 0.0 copy-start
  0.6 1.3 %copy_bitcast_fusion = (bf16[2,64,1536]{2,1,0:T(8,128)(2,1)S(1)}, bf16[2,64,1536]{2,1,0:T(8,128)(2,1)S(1)}) fusion(bf16[64,2,1536]{2,1,0:T(2,128)(2,1)} %param.5, bf16[64,2,1536]{2,1,0:T(2,128)(2,1)} %param.3), kind=kLoop, calls=%fused_computation | loop fusion | bytes 1572864 | tf_op jit(solution)/shard_map/transpose | solution.py:372
  1.9 0.1 copy-done
  2.0 79.0 %shard_map.58 = (bf16[2,64,1536]{2,1,0:T(8,128)(2,1)S(1)}, bf16[2,64,1536]{2,1,0:T(8,128)(2,1)S(1)}, f32[27,32,64]{2,1,0:T(8,128)S(1)}) custom-call(bf16[2,64,1536]{2,1,0:T(8,128)(2,1)S(1)} %get-tuple-element.13.x, bf16[2,64,1536]{2,1,0:T(8,128)(2,1)S(1)} %get-tuple-element.12.g, bf16[27,64,256]{2,1,0:T(8,128)(2,1)S(1)} %copy-done), custom_call_target="tpu_custom_call" | custom-call | tf_op jit(solution)/shard_map/pallas_call | solution.py:375
  81.0 1.2 %copy.8 = bf16[64,2,1536]{2,1,0:T(2,128)(2,1)} copy(bf16[64,2,1536]{2,0,1:T(8,128)(2,1)S(1)} %bitcast.9) | data formatting | bytes 786432
  82.1 1.1 %copy.9 = bf16[64,2,1536]{2,1,0:T(2,128)(2,1)} copy(bf16[64,2,1536]{2,0,1:T(8,128)(2,1)S(1)} %bitcast.8) | data formatting | bytes 786432
  83.3 0.8 copy.13
Async XLA Ops:
  0.6 1.4 %copy-start = (bf16[27,64,256]{2,1,0:T(8,128)(2,1)S(1)}, bf16[27,64,256]{2,1,0:T(8,128)(2,1)}, u32[]{:S(2)}) copy-start(bf16[27,64,256]{2,1,0:T(8,128)(2,1)} %w.1) | copy-start | bytes 2654212
